TPU v7x, 256 devices: a whole 4x4x8 slice. The times are simulated.
256 devices in a mesh: region: 16 (over x, y_lo, core), rows: 16 (over y_hi, z).
Axes of the slice: x: 4, y: 4 (y_hi: 2, y_lo: 2; y = y_hi * 2 + y_lo), z: 8, core: 2. Of those that a mesh axis runs over, the one named last changes fastest.
Arguments:
- basis_values: bfloat16 [393216, 1024], P(('region', 'rows')), may hold values from -6 to 6
- grid_weights: float32 [393216], P(('region', 'rows')), may hold values from 0.0076546553 to 0.07654656
- density_blocks: bfloat16 [131072, 512], P(('region', 'rows')), may hold values from -0.046875 to 0.046875
- pattern: int32 [2048, 8], replicated, may hold values from 0 to 2047, as said below
- active: int32 [256, 16], replicated, may hold values from 0 to 2047, as said below
Outputs:
- density: float32 [393216], P(('region', 'rows'))
- hamiltonian: float32 [131072, 512], P(('region', 'rows'))
Inputs may be any that keep to these rules, and one draw needn't show every extreme that they name: `pattern`: block row a names 8 distinct blocks, a itself among them. `active`: block id g lies in region g // 128 and belongs to row index (g // 8) % 16. Batch b lies in region b // 16; its list holds 16 distinct blocks: entries 0 to 7 in its region, the next 4 in the region before it, the last 4 in the region after it (regions counted modulo 16). At most 2 entries of one list belong to one row index, and in every list some row index holds exactly 2.
All inputs are finite; a program needn't handle non-finite values.
Results may differ from a plain program's by a relative error of at most 0.0055.
Values may be sent and summed in bfloat16 or wider, within the bound.
A program may use at most 64 MiB of HBM per device.

v0:
```python
import jax
import jax.numpy as jnp
from jax import lax
from jax.sharding import PartitionSpec as P

BS = 64
BLK_DEV = 8
KNZ = 8
ACT = 16


def with_halo(array, sides, width):
    for axis, dim in sides:
        size, length = (lax.axis_size(axis), array.shape[dim])
        up = [(i, (i + 1) % size) for i in range(size)]
        down = [(j, i) for i, j in up]
        last = lax.slice_in_dim(array, length - width, length, axis=dim)
        leading = lax.slice_in_dim(array, 0, width, axis=dim)
        before = lax.ppermute(last, axis, up)
        after = lax.ppermute(leading, axis, down)
        array = jnp.concatenate([before, array, after], axis=dim)
    return array


def shifted(block, axis, distance):
    devices = range(lax.axis_size(axis))
    route = [((i - distance) % len(devices), i) for i in devices]
    return lax.ppermute(block, axis, route)


def shards(basis_values, grid_weights, density_blocks, pattern, active):
    row_count = lax.axis_size("rows")
    region_count = lax.axis_size("region")
    region_here = lax.axis_index("region")
    row_here = lax.axis_index("rows")
    capacity = (ACT - 2) // row_count + 2
    blocks_region = BLK_DEV * row_count
    slot_total = row_count * capacity
    stored_width = KNZ * BS
    batch_width = ACT * BS
    extended = with_halo(density_blocks, (("region", 0),), BLK_DEV * BS)
    extended = extended.reshape(3 * BLK_DEV, BS, stored_width)
    targets = lax.dynamic_slice_in_dim(active, region_here * row_count, row_count, 0)
    owners = targets // BLK_DEV % row_count
    groups = (targets // blocks_region - region_here + 1) % region_count
    local_rows = groups * BLK_DEV + targets % BLK_DEV
    owned_here = (owners == row_here).astype(jnp.int32)
    earlier = jnp.cumsum(owned_here, axis=1) - owned_here
    slot_numbers = jnp.arange(capacity, dtype=jnp.int32)
    slot_pick = owned_here[:, None, :] * (
        earlier[:, None, :] == slot_numbers[None, :, None]
    ).astype(jnp.int32)
    filled = jnp.sum(slot_pick, axis=2).reshape(slot_total)
    slot_rows = jnp.sum(slot_pick * local_rows[:, None, :], axis=2).reshape(slot_total)
    picked = jnp.where(filled[:, None, None] > 0, extended[slot_rows], jnp.zeros((), jnp.bfloat16))
    outgoing = picked.reshape(row_count, capacity, BS, stored_width)
    received = lax.all_to_all(outgoing, "rows", split_axis=0, concat_axis=0, tiled=True)
    wire_width = received.shape[3]
    received = received.reshape(slot_total, BS, wire_width)
    batch_ids = lax.dynamic_slice_in_dim(active, region_here * row_count + row_here, 1, 0)[0]
    batch_owners = batch_ids // BLK_DEV % row_count
    entry_order = jnp.arange(ACT, dtype=jnp.int32)
    same_before = (batch_owners[:, None] == batch_owners[None, :]) & (
        entry_order[:, None] > entry_order[None, :]
    )
    arrivals = batch_owners * capacity + jnp.sum(same_before.astype(jnp.int32), axis=1)
    entry_rows = received[arrivals]
    batch_match = (pattern[batch_ids][:, :, None] == batch_ids[None, None, :]).astype(jnp.bfloat16)
    sub_density = jnp.einsum(
        "krmc,kmj->krjc",
        entry_rows.reshape(ACT, BS, KNZ, BS),
        batch_match,
        preferred_element_type=jnp.float32,
    )
    sub_density = sub_density.astype(jnp.bfloat16).reshape(batch_width, batch_width)
    product = jnp.dot(basis_values, sub_density, preferred_element_type=jnp.float32)
    density = jnp.sum(product * basis_values, axis=1)
    scaled = (basis_values * (grid_weights * jnp.tanh(density))[:, None]).astype(jnp.bfloat16)
    batch_ham = lax.dot_general(
        scaled, basis_values, (((0,), (0,)), ((), ())), preferred_element_type=jnp.float32
    ).astype(jnp.bfloat16)
    ham_rows = jnp.einsum(
        "krjc,kmj->krmc",
        batch_ham.reshape(ACT, BS, ACT, BS),
        batch_match,
        preferred_element_type=jnp.float32,
    )
    ham_rows = ham_rows.astype(jnp.bfloat16).reshape(ACT, BS, stored_width)
    sending = jnp.zeros((slot_total, BS, wire_width), jnp.bfloat16).at[arrivals].set(ham_rows)
    returned = lax.all_to_all(
        sending.reshape(row_count, capacity, BS, wire_width),
        "rows",
        split_axis=0,
        concat_axis=0,
        tiled=True,
    )
    returned = returned.reshape(slot_total, BS, wire_width)
    pieces = returned.reshape(slot_total, BS * stored_width)
    row_numbers = jnp.arange(3 * BLK_DEV, dtype=jnp.int32)
    placing = ((slot_rows[None, :] == row_numbers[:, None]) & (filled[None, :] > 0)).astype(
        jnp.bfloat16
    )
    grouped = jnp.dot(placing, pieces, preferred_element_type=jnp.float32).reshape(
        3, BLK_DEV * BS, stored_width
    )
    from_right = shifted(grouped[0].astype(jnp.bfloat16), "region", -1).astype(jnp.float32)
    from_left = shifted(grouped[2].astype(jnp.bfloat16), "region", 1).astype(jnp.float32)
    return (density, grouped[1] + from_right + from_left)


def solution(mesh):
    placed = (
        P(("region", "rows"), None),
        P(("region", "rows")),
        P(("region", "rows"), None),
        P(),
        P(),
    )
    return jax.shard_map(
        shards,
        mesh=mesh,
        in_specs=placed,
        out_specs=(P(("region", "rows")), P(("region", "rows"), None)),
        check_vma=False,
    )
```

profile of v0, /device:TPU:1, one launch (start us, length us, event | category | flops | bytes accessed | tf_op | source)
XLA Modules:
  0.0 196.8 jit_solution(14637901663568486774)
XLA Ops:
  0.6 2.8 %collective-permute-start = (bf16[512,512]{1,0:T(8,128)(2,1)}, bf16[512,512]{1,0:T(8,128)(2,1)S(1)}, u32[]{:S(2)}, u32[]{:S(2)}) collective-permute-start(bf16[512,512]{1,0:T(8,128)(2,1)} %param.7), channel_id=1, source_target_pairs={{0,16},{16,32},{32,48},{48,64},{64,80},{80,96},{96,112},{112,128},... | collective-permute-start | bytes 1572872 | tf_op jit(solution)/shard_map/ppermute | solution.py:19
  5.6 9.9 %collective-permute-done = bf16[512,512]{1,0:T(8,128)(2,1)S(1)} collective-permute-done((bf16[512,512]{1,0:T(8,128)(2,1)}, bf16[512,512]{1,0:T(8,128)(2,1)S(1)}, u32[]{:S(2)}, u32[]{:S(2)}) %collective-permute-start) | collective-permute-done | bytes 524320 | tf_op jit(solution)/shard_map/ppermute | solution.py:19
  15.5 2.4 %collective-permute-done.1 = bf16[512,512]{1,0:T(8,128)(2,1)S(1)} collective-permute-done((bf16[512,512]{1,0:T(8,128)(2,1)}, bf16[512,512]{1,0:T(8,128)(2,1)S(1)}, u32[]{:S(2)}, u32[]{:S(2)}) %collective-permute-start.1) | collective-permute-done | bytes 524320 | tf_op jit(solution)/shard_map/ppermute | solution.py:20
  19.0 2.0 %gather_fusion.1 = bf16[32,64,512]{2,1,0:T(8,128)(2,1)} fusion(bf16[24,64,512]{2,1,0:T(8,128)(2,1)S(1)} %bitcast.53, s32[1024]{0:T(1024)S(1)} %pad_clamp_fusion.1), kind=kCustom, calls=%fused_computation.1 | custom fusion | bytes 4194432 | tf_op jit(solution)/shard_map/gather | solution.py:55
  20.9 3.1 %broadcast_select_fusion = bf16[16,2,64,512]{3,2,1,0:T(8,128)(2,1)} fusion(bf16[16,2,64,512]{3,2,1,0:T(8,128)(2,1)} %bitcast.56, pred[16,2]{1,0:T(8,128)(4,1)S(1)} %copy.15), kind=kLoop, calls=%fused_computation.12 | loop fusion | flops 1048576 | bytes 4194336 | tf_op jit(solution)/shard_map/jit(_where)/select_n | solution.py:55
  24.1 10.8 %all-to-all-start = ((bf16[16,2,64,512]{3,2,1,0:T(8,128)(2,1)}), bf16[16,2,64,512]{3,2,1,0:T(8,128)(2,1)S(1)}, u32[]{:S(2)}, u32[]{:S(2)}) async-start(bf16[16,2,64,512]{3,2,1,0:T(8,128)(2,1)} %broadcast_select_fusion), calls=%async_computation | async-start | bytes 4194304 | tf_op jit(solution)/shard_map/all_to_all | solution.py:57
  35.2 4.7 %copy.17 = bf16[1536,1024]{0,1:T(8,128)(2,1)} copy(bf16[1536,1024]{1,0:T(8,128)(2,1)} %param.5) | data formatting | bytes 6291456 | tf_op args[0]
  40.9 41.5 %all-to-all-done = bf16[16,2,64,512]{3,2,1,0:T(8,128)(2,1)S(1)} async-done(((bf16[16,2,64,512]{3,2,1,0:T(8,128)(2,1)}), bf16[16,2,64,512]{3,2,1,0:T(8,128)(2,1)S(1)}, u32[]{:S(2)}, u32[]{:S(2)}) %all-to-all-start) | async-done | bytes 2097184 | tf_op jit(solution)/shard_map/all_to_all | solution.py:57
  84.2 3.0 %convert_bitcast_fusion = bf16[16,64,16,64]{3,2,1,0:T(8,128)(2,1)} fusion(bf16[16,64,8,64]{3,2,1,0:T(8,128)(2,1)S(1)} %reshape.247, s32[16]{0:T(128)S(1)} %get-tuple-element.2, s32[16,8]{1,0:T(8,128)S(1)} %gather_fusion), kind=kOutput, calls=%fused_computation.8 | convolution fusion | flops 17827840 | bytes 3146304 | tf_op jit(solution)/shard_map/krmc,kmj->krjc/dot_general | solution.py:69
  87.1 6.7 %reshape.248 = bf16[1024,1024]{1,0:T(8,128)(2,1)} reshape(bf16[16,64,16,64]{3,2,1,0:T(8,128)(2,1)} %convert_bitcast_fusion) | data formatting | bytes 4194304 | tf_op jit(solution)/shard_map/reshape | solution.py:75
  93.8 6.0 %fusion = f32[1536]{0:T(1024)S(1)} fusion(bf16[1536,1024]{0,1:T(8,128)(2,1)} %copy.17, bf16[1024,1024]{1,0:T(8,128)(2,1)} %reshape.248, bf16[1536,1024]{1,0:T(8,128)(2,1)S(1)} %copy-done), kind=kOutput, calls=%fused_computation.6 | convolution fusion | flops 3225942528 | bytes 8394752 | tf_op jit(solution)/shard_map/dot_general | solution.py:76
  99.8 4.7 %fusion.5 = bf16[1024,1024]{1,0:T(8,128)(2,1)} fusion(bf16[1536,1024]{1,0:T(8,128)(2,1)S(1)} %copy-done, bf16[1536,1024]{0,1:T(8,128)(2,1)S(1)} %copy-done.1, f32[1536]{0:T(1024)S(1)} %tanh_multiply_fusion), kind=kOutput, calls=%fused_computation.13 | convolution fusion | flops 3226992640 | bytes 8394752 | tf_op jit(solution)/shard_map/dot_general | solution.py:79
  104.5 6.4 %reshape.249 = bf16[16,64,16,64]{3,2,1,0:T(8,128)(2,1)} reshape(bf16[1024,1024]{1,0:T(8,128)(2,1)} %fusion.5) | data formatting | bytes 4194304 | tf_op jit(solution)/shard_map/reshape | solution.py:84
  110.9 2.9 %convert_bitcast_fusion.1 = bf16[16,64,8,64]{3,2,1,0:T(8,128)(2,1)S(1)} fusion(bf16[16,64,16,64]{3,2,1,0:T(8,128)(2,1)} %reshape.249, s32[16]{0:T(128)S(1)} %get-tuple-element.2, s32[16,8]{1,0:T(8,128)S(1)} %gather_fusion), kind=kOutput, calls=%fused_computation.11 | convolution fusion | flops 17303552 | bytes 3146304 | tf_op jit(solution)/shard_map/krjc,kmj->krmc/dot_general | solution.py:82
  113.8 1.3 reshape.280
  115.1 1.6 broadcast_in_dim.16
  116.7 3.0 %scatter_fusion = bf16[32,64,512]{2,1,0:T(8,128)(2,1)} fusion(bf16[32,64,512]{2,1,0:T(8,128)(2,1)} %broadcast_in_dim.16, s32[16]{0:T(128)S(1)} %get-tuple-element.9, bf16[16,64,512]{2,1,0:T(8,128)(2,1)S(1)} %reshape.280), kind=kCustom, calls=%fused_computation.3 | custom fusion | bytes 3145792 | tf_op jit(solution)/shard_map/scatter | solution.py:89
  119.7 4.4 %all-to-all-start.1 = ((bf16[16,2,64,512]{3,2,1,0:T(8,128)(2,1)}), bf16[16,2,64,512]{3,2,1,0:T(8,128)(2,1)S(1)}, u32[]{:S(2)}, u32[]{:S(2)}) async-start(bf16[16,2,64,512]{3,2,1,0:T(8,128)(2,1)} %bitcast.13), calls=%async_computation.1 | async-start | bytes 4194304 | tf_op jit(solution)/shard_map/all_to_all | solution.py:90
  124.2 50.7 %all-to-all-done.1 = bf16[16,2,64,512]{3,2,1,0:T(8,128)(2,1)S(1)} async-done(((bf16[16,2,64,512]{3,2,1,0:T(8,128)(2,1)}), bf16[16,2,64,512]{3,2,1,0:T(8,128)(2,1)S(1)}, u32[]{:S(2)}, u32[]{:S(2)}) %all-to-all-start.1) | async-done | bytes 2097184 | tf_op jit(solution)/shard_map/all_to_all | solution.py:90
  177.7 2.1 %convert_element_type.54 = bf16[512,512]{1,0:T(8,128)(2,1)} reshape(bf16[8,32768]{1,0:T(8,128)(2,1)} %get-tuple-element.6) | data formatting | bytes 1048576 | tf_op jit(solution)/shard_map/convert_element_type | solution.py:106
  180.6 2.1 %convert_element_type.56 = bf16[512,512]{1,0:T(8,128)(2,1)} reshape(bf16[8,32768]{1,0:T(8,128)(2,1)} %get-tuple-element.7) | data formatting | bytes 1048576 | tf_op jit(solution)/shard_map/convert_element_type | solution.py:107
  184.7 1.4 squeeze.9
  186.1 8.2 %collective-permute-done.2 = bf16[512,512]{1,0:T(8,128)(2,1)} collective-permute-done((bf16[512,512]{1,0:T(8,128)(2,1)}, bf16[512,512]{1,0:T(8,128)(2,1)}, u32[]{:S(2)}, u32[]{:S(2)}) %collective-permute-start.2) | collective-permute-done | bytes 524320 | tf_op jit(solution)/shard_map/ppermute | solution.py:28
  194.4 2.4 %convert_add_fusion = f32[512,512]{1,0:T(8,128)} fusion(bf16[512,512]{1,0:T(8,128)(2,1)} %collective-permute-done.3, f32[512,512]{1,0:T(8,128)S(1)} %squeeze.9, bf16[512,512]{1,0:T(8,128)(2,1)} %collective-permute-done.2), kind=kLoop, calls=%fused_computation.15 | loop fusion | flops 1048576 | bytes 3145728 | tf_op jit(solution)/shard_map/add | solution.py:108
  (46 shorter events, 12.1 us)
Async XLA Ops:
  0.6 14.8 %collective-permute-start = (bf16[512,512]{1,0:T(8,128)(2,1)}, bf16[512,512]{1,0:T(8,128)(2,1)S(1)}, u32[]{:S(2)}, u32[]{:S(2)}) collective-permute-start(bf16[512,512]{1,0:T(8,128)(2,1)} %param.7), channel_id=1, source_target_pairs={{0,16},{16,32},{32,48},{48,64},{64,80},{80,96},{96,112},{112,128},... | collective-permute-start | bytes 1572872 | tf_op jit(solution)/shard_map/ppermute | solution.py:19
  3.4 14.4 %collective-permute-start.1 = (bf16[512,512]{1,0:T(8,128)(2,1)}, bf16[512,512]{1,0:T(8,128)(2,1)S(1)}, u32[]{:S(2)}, u32[]{:S(2)}) collective-permute-start(bf16[512,512]{1,0:T(8,128)(2,1)} %param.7), channel_id=1, source_target_pairs={{16,0},{32,16},{48,32},{64,48},{80,64},{96,80},{112,96},{128,112},... | collective-permute-start | bytes 1572872 | tf_op jit(solution)/shard_map/ppermute | solution.py:20
  24.1 10.8 %copy-start.2 = (s32[2048,8]{0,1:T(8,128)S(1)}, s32[2048,8]{0,1:T(8,128)}, u32[]{:S(2)}) copy-start(s32[2048,8]{0,1:T(8,128)} %param.8) | copy-start | bytes 196612
  24.1 58.3 %all-to-all-start = ((bf16[16,2,64,512]{3,2,1,0:T(8,128)(2,1)}), bf16[16,2,64,512]{3,2,1,0:T(8,128)(2,1)S(1)}, u32[]{:S(2)}, u32[]{:S(2)}) async-start(bf16[16,2,64,512]{3,2,1,0:T(8,128)(2,1)} %broadcast_select_fusion), calls=%async_computation | async-start | bytes 4194304 | tf_op jit(solution)/shard_map/all_to_all | solution.py:57
  35.2 4.7 %copy-start.3 = (s32[256,16]{0,1:T(8,128)S(1)}, s32[256,16]{0,1:T(8,128)}, u32[]{:S(2)}) copy-start(s32[256,16]{0,1:T(8,128)} %param.9) | copy-start | bytes 49156
  87.1 6.7 %copy-start = (bf16[1536,1024]{1,0:T(8,128)(2,1)S(1)}, bf16[1536,1024]{1,0:T(8,128)(2,1)}, u32[]{:S(2)}) copy-start(bf16[1536,1024]{1,0:T(8,128)(2,1)} %param.5) | copy-start | bytes 9437188
  93.8 6.0 %copy-start.4 = (f32[1536]{0:T(1024)S(1)}, f32[1536]{0:T(1024)}, u32[]{:S(2)}) copy-start(f32[1536]{0:T(1024)} %param.6) | copy-start | bytes 18436
  93.8 6.0 %copy-start.1 = (bf16[1536,1024]{0,1:T(8,128)(2,1)S(1)}, bf16[1536,1024]{0,1:T(8,128)(2,1)}, u32[]{:S(2)}) copy-start(bf16[1536,1024]{0,1:T(8,128)(2,1)} %copy.17) | copy-start | bytes 9437188
  99.8 4.7 %copy-start.5 = (f32[1536]{0:T(1024)}, f32[1536]{0:T(1024)S(1)}, u32[]{:S(2)}) copy-start(f32[1536]{0:T(1024)S(1)} %fusion) | copy-start | bytes 18436
  119.7 55.3 %all-to-all-start.1 = ((bf16[16,2,64,512]{3,2,1,0:T(8,128)(2,1)}), bf16[16,2,64,512]{3,2,1,0:T(8,128)(2,1)S(1)}, u32[]{:S(2)}, u32[]{:S(2)}) async-start(bf16[16,2,64,512]{3,2,1,0:T(8,128)(2,1)} %bitcast.13), calls=%async_computation.1 | async-start | bytes 4194304 | tf_op jit(solution)/shard_map/all_to_all | solution.py:90
  179.8 14.5 %collective-permute-start.2 = (bf16[512,512]{1,0:T(8,128)(2,1)}, bf16[512,512]{1,0:T(8,128)(2,1)}, u32[]{:S(2)}, u32[]{:S(2)}) collective-permute-start(bf16[512,512]{1,0:T(8,128)(2,1)} %convert_element_type.54), channel_id=1, source_target_pairs={{16,0},{32,16},{48,32},{64,48},{80,64},{96,80},{112,96},{128,112},... | collective-permute-start | bytes 1572872 | tf_op jit(solution)/shard_map/ppermute | solution.py:28
  182.7 11.7 %collective-permute-start.3 = (bf16[512,512]{1,0:T(8,128)(2,1)}, bf16[512,512]{1,0:T(8,128)(2,1)}, u32[]{:S(2)}, u32[]{:S(2)}) collective-permute-start(bf16[512,512]{1,0:T(8,128)(2,1)} %convert_element_type.56), channel_id=1, source_target_pairs={{240,0},{0,16},{16,32},{32,48},{48,64},{64,80},{80,96},{96,112},{1... | collective-permute-start | bytes 1572872 | tf_op jit(solution)/shard_map/ppermute | solution.py:28
where the time goes:
time: 198 us; the launch traced here: 197 us
  waiting for transfers between devices  113 us (57%)
  local copies, waits for them, and re-layouts  38.3 us (19%)
  starting transfers between devices  20.3 us (10%)
  matrix products  17.1 us (9%)
  other arithmetic  7.5 us (4%)
    all_to_all x1, waiting for transfers between devices, shards(): lax.all_to_all(sending.reshape(row_count, capacity, BS, wire_width), 'row...  50.7 us
    all_to_all x1, waiting for transfers between devices, shards(): lax.all_to_all(outgoing, 'rows', split_axis=0, concat_axis=0, tiled=True)  41.5 us
    all_to_all x1, starting transfers between devices, shards(): lax.all_to_all(outgoing, 'rows', split_axis=0, concat_axis=0, tiled=True)  10.8 us
    ppermute x1, waiting for transfers between devices, with_halo(): before = lax.ppermute(last, axis, up)  9.87 us
    ppermute x2, waiting for transfers between devices, shifted(): return lax.ppermute(block, axis, route)  8.25 us
    reshape x1, local copies, waits for them, and re-layouts, shards(): sub_density.astype(jnp.bfloat16).reshape(batch_width, batch_width)  6.67 us
    reshape x1, local copies, waits for them, and re-layouts, shards(): batch_ham.reshape(ACT, BS, ACT, BS)  6.37 us
    unnamed x16, local copies, waits for them, and re-layouts  6.26 us
  transfers between devices with their start and end apart: 6, of which 5 were waited for; matrix products, arithmetic and copies ran while one was open for 6% of the time, Pallas kernels for 0%

commit v1 on v0

v1 whole, which is shorter than its diff:
```python
import functools

import jax
import jax.numpy as jnp
from jax import lax
from jax.experimental import pallas as pl
from jax.experimental.pallas import tpu as pltpu
from jax.sharding import PartitionSpec as P

BS = 64
BLK_DEV = 8
KNZ = 8
ACT = 16
PTS = 1536
ROWS = 16
WIDTH = KNZ * BS
COLS = ACT * BS
CHUNK = 256
MESH = pl.DeviceIdType.MESH
F32 = jnp.float32
BF16 = jnp.bfloat16
PEERS = tuple(
    (dy, dz)
    for dz in (4, 3, 5, 2, 6, 1, 7, 0)
    for dy in (0, 1)
    if (dy, dz) != (0, 0)
)


def half_masks():
    lane = lax.broadcasted_iota(jnp.int32, (BS, 128), 1)
    low = jnp.where(lane < BS, 1.0, 0.0).astype(BF16)
    high = jnp.where(lane < BS, 0.0, 1.0).astype(BF16)
    return low, high


def pair_of_blocks(source, row, first, second, masks):
    low, high = masks
    a = source[first & 1, row, first >> 1]
    b = source[1 - (second & 1), row, second >> 1]
    return a * low + b * high


def swap_halves(values):
    return pltpu.roll(values, 64, 1)


def kernel(
    act, pat, weights, x_hbm, d_hbm,
    dens_out, ham_out,
    xv, xt, ext, send_d, recv_d, rows2, dfull, svec, hrows, send_h, recv_h,
    halo_out, halo_in,
    tab_row, tab_arr, tab_m, tab_j, tab_slot,
    local_sems, halo_send, halo_recv, a2a_send, a2a_recv,
):
    g = lax.axis_index("region")
    me = lax.axis_index("rows")
    y = lax.div(me, 8)
    z = lax.rem(me, 8)
    left, right = lax.rem(g + 15, 16), lax.rem(g + 1, 16)

    def peer(dy, dz):
        return lax.rem(y + dy, 2) * 8 + lax.rem(z + dz, 8)

    x_copy = pltpu.make_async_copy(x_hbm, xv, local_sems.at[0])
    x_copy.start()
    d_copy = pltpu.make_async_copy(d_hbm, ext.at[pl.ds(BLK_DEV, BLK_DEV)], local_sems.at[1])
    d_copy.start()

    barrier = pltpu.get_barrier_semaphore()
    for n in (left, right):
        pl.semaphore_signal(barrier, inc=1, device_id=(n, me), device_id_type=MESH)
    for dy, dz in PEERS:
        pl.semaphore_signal(barrier, inc=1, device_id=(g, peer(dy, dz)), device_id_type=MESH)
    pl.semaphore_wait(barrier, 17)

    to_right = pltpu.make_async_remote_copy(
        d_hbm, ext.at[pl.ds(0, BLK_DEV)], halo_send.at[0], halo_recv.at[0],
        device_id=(right, me), device_id_type=MESH)
    to_left = pltpu.make_async_remote_copy(
        d_hbm, ext.at[pl.ds(2 * BLK_DEV, BLK_DEV)], halo_send.at[1], halo_recv.at[1],
        device_id=(left, me), device_id_type=MESH)
    to_right.start()
    to_left.start()

    def rows_of_batch(b, carry):
        first = jnp.int32(0)
        second = jnp.int32(0)
        count = jnp.int32(0)
        for e in range(ACT):
            block = act[e, g * ROWS + b]
            mine = ((block >> 3) & (ROWS - 1)) == me
            row = jnp.minimum(((block >> 7) - g + 1) & 15, 2) * BLK_DEV + (block & 7)
            first = jnp.where(mine & (count == 0), row, first)
            second = jnp.where(mine & (count == 1), row, second)
            count = count + mine.astype(jnp.int32)
        tab_row[2 * b] = first
        tab_row[2 * b + 1] = second
        tab_row[2 * ROWS + b] = count
        return carry

    lax.fori_loop(0, ROWS, rows_of_batch, 0)

    d_copy.wait()
    to_right.wait_recv()
    to_left.wait_recv()

    first_copies = []
    for i, (dy, dz) in enumerate(PEERS):
        p = peer(dy, dz)
        for c in range(2):
            send_d[p, c] = ext[tab_row[2 * p + c]]
        copy = pltpu.make_async_remote_copy(
            send_d.at[p], recv_d.at[pl.ds(2 * me, 2)], a2a_send.at[i], a2a_recv.at[i],
            device_id=(g, p), device_id_type=MESH)
        copy.start()
        first_copies.append(copy)
    for c in range(2):
        recv_d[2 * me + c] = ext[tab_row[2 * me + c]]

    ids = [act[k, g * ROWS + me] for k in range(ACT)]
    owners = [(i >> 3) & (ROWS - 1) for i in ids]
    for k in range(ACT):
        earlier = jnp.int32(0)
        for j in range(k):
            earlier = earlier + (owners[j] == owners[k]).astype(jnp.int32)
        tab_arr[k] = owners[k] * 2 + jnp.minimum(earlier, 1)

    def slot_entries(s, carry):
        entry = jnp.int32(0)
        for k in range(ACT):
            entry = jnp.where(tab_arr[k] == s, k, entry)
        tab_slot[s] = entry
        return carry

    lax.fori_loop(0, 2 * ROWS, slot_entries, 0)

    def match_row(k, carry):
        block = act[k, g * ROWS + me]
        found_m = [jnp.int32(KNZ)] * ACT
        for m in range(KNZ):
            column = pat[m, block]
            found = jnp.int32(ACT)
            for j in range(ACT):
                same = column == act[j, g * ROWS + me]
                found = jnp.where(same, j, found)
                found_m[j] = jnp.where(same, m, found_m[j])
            tab_j[k * KNZ + m] = found
        for j in range(ACT):
            tab_m[k * ACT + j] = found_m[j]
        return carry

    lax.fori_loop(0, ACT, match_row, 0)

    rows2[:, :, KNZ // 2] = jnp.zeros((2, ACT, BS, 128), BF16)
    hrows[:, :, ACT // 2] = jnp.zeros((2, ACT, BS, 128), BF16)
    recv_h[:, 2] = jnp.zeros((ROWS, BS, WIDTH), BF16)

    x_copy.wait()

    def transpose_chunk(i, carry):
        points = pl.ds(pl.multiple_of(i * 128, 128), 128)
        xt[:, points] = jnp.transpose(xv[points, :])
        return carry

    lax.fori_loop(0, PTS // 128, transpose_chunk, 0)

    masks = half_masks()
    for copy in first_copies:
        copy.wait_recv()

    def spread_row(k, carry):
        row = recv_d[tab_arr[k]]
        for q in range(KNZ // 2):
            part = row[:, q * 128 : (q + 1) * 128]
            rows2[0, k, q] = part
            rows2[1, k, q] = swap_halves(part.astype(F32)).astype(BF16)
        for q in range(ACT // 2):
            first = tab_m[k * ACT + 2 * q]
            second = tab_m[k * ACT + 2 * q + 1]
            dfull[pl.ds(pl.multiple_of(k * BS, BS), BS), q * 128 : (q + 1) * 128] = pair_of_blocks(
                rows2, k, first, second, masks)
        return carry

    lax.fori_loop(0, ACT, spread_row, 0)

    def density_chunk(i, carry):
        points = pl.ds(pl.multiple_of(i * CHUNK, CHUNK), CHUNK)
        x = xv[points, :]
        part = jnp.zeros((CHUNK, 128), F32)
        for n in range(COLS // CHUNK):
            product = jnp.dot(x, dfull[:, n * CHUNK : (n + 1) * CHUNK], preferred_element_type=F32)
            product = product * x[:, n * CHUNK : (n + 1) * CHUNK].astype(F32)
            part = part + (product[:, :128] + product[:, 128:])
        dens = jnp.sum(jnp.transpose(part), axis=0, keepdims=True)
        dens_out[:, points] = dens
        svec[:, points] = weights[:, points] * jnp.tanh(dens)
        return carry

    lax.fori_loop(0, PTS // CHUNK, density_chunk, 0)

    def ham_chunk(i, carry):
        scaled = (xt[pl.ds(pl.multiple_of(i * CHUNK, CHUNK), CHUNK), :].astype(F32) * svec[...]).astype(BF16)
        for n in range(COLS // CHUNK):
            block = jnp.dot(scaled, xv[:, n * CHUNK : (n + 1) * CHUNK], preferred_element_type=F32)
            for half in range(CHUNK // 128):
                part = block[:, half * 128 : (half + 1) * 128]
                swapped = swap_halves(part).astype(BF16)
                part = part.astype(BF16)
                for kk in range(CHUNK // BS):
                    entry = i * (CHUNK // BS) + kk
                    hrows[0, entry, 2 * n + half] = part[kk * BS : (kk + 1) * BS]
                    hrows[1, entry, 2 * n + half] = swapped[kk * BS : (kk + 1) * BS]
        return carry

    lax.fori_loop(0, COLS // CHUNK, ham_chunk, 0)

    for copy in first_copies:
        copy.wait_send()

    def gather_slots(p, target, target_row):
        for c in range(2):
            k = tab_slot[2 * p + c]
            for q in range(KNZ // 2):
                first = tab_j[k * KNZ + 2 * q]
                second = tab_j[k * KNZ + 2 * q + 1]
                target[target_row, c, :, q * 128 : (q + 1) * 128] = pair_of_blocks(
                    hrows, k, first, second, masks)

    second_copies = []
    for i, (dy, dz) in enumerate(PEERS):
        p = peer(dy, dz)
        gather_slots(p, send_h, p)
        copy = pltpu.make_async_remote_copy(
            send_h.at[p], recv_h.at[me, pl.ds(0, 2)], a2a_send.at[15 + i], a2a_recv.at[15 + i],
            device_id=(g, p), device_id_type=MESH)
        copy.start()
        second_copies.append(copy)
    gather_slots(me, recv_h, me)
    for copy in second_copies:
        copy.wait_recv()

    def sum_row(t):
        picks = []
        for b in range(ROWS):
            count = tab_row[2 * ROWS + b]
            picks.append(jnp.where(
                (tab_row[2 * b] == t) & (count > 0), 0,
                jnp.where((tab_row[2 * b + 1] == t) & (count > 1), 1, 2)))
        total = recv_h[0, picks[0]].astype(F32)
        for b in range(1, ROWS):
            total = total + recv_h[b, picks[b]].astype(F32)
        return total

    def side_row(t, carry):
        for side, base in ((0, 0), (1, 2 * BLK_DEV)):
            halo_out[side, t] = sum_row(base + t).astype(BF16)
        return carry

    lax.fori_loop(0, BLK_DEV, side_row, 0)

    back_left = pltpu.make_async_remote_copy(
        halo_out.at[0], halo_in.at[0], halo_send.at[2], halo_recv.at[2],
        device_id=(left, me), device_id_type=MESH)
    back_right = pltpu.make_async_remote_copy(
        halo_out.at[1], halo_in.at[1], halo_send.at[3], halo_recv.at[3],
        device_id=(right, me), device_id_type=MESH)
    back_left.start()
    back_right.start()

    def own_row(t, carry):
        ham_out[t] = sum_row(BLK_DEV + t)
        return carry

    lax.fori_loop(0, BLK_DEV, own_row, 0)
    back_left.wait_recv()
    back_right.wait_recv()

    def add_row(t, carry):
        ham_out[t] = ham_out[t] + halo_in[0, t].astype(F32) + halo_in[1, t].astype(F32)
        return carry

    lax.fori_loop(0, BLK_DEV, add_row, 0)

    for copy in second_copies:
        copy.wait_send()
    for copy in (to_right, to_left, back_left, back_right):
        copy.wait_send()


def shards(basis_values, grid_weights, density_blocks, pattern, active):
    vmem = pl.BlockSpec(memory_space=pltpu.VMEM)
    smem = pl.BlockSpec(memory_space=pltpu.SMEM)
    hbm = pl.BlockSpec(memory_space=pl.ANY)
    dens, ham = pl.pallas_call(
        kernel,
        out_shape=(
            jax.ShapeDtypeStruct((1, PTS), F32),
            jax.ShapeDtypeStruct((BLK_DEV, BS, WIDTH), F32),
        ),
        in_specs=[smem, smem, vmem, hbm, hbm],
        out_specs=(vmem, vmem),
        scratch_shapes=[
            pltpu.VMEM((PTS, COLS), BF16),
            pltpu.VMEM((COLS, PTS), BF16),
            pltpu.VMEM((3 * BLK_DEV, BS, WIDTH), BF16),
            pltpu.VMEM((ROWS, 2, BS, WIDTH), BF16),
            pltpu.VMEM((2 * ROWS, BS, WIDTH), BF16),
            pltpu.VMEM((2, ACT, KNZ // 2 + 1, BS, 128), BF16),
            pltpu.VMEM((COLS, COLS), BF16),
            pltpu.VMEM((1, PTS), F32),
            pltpu.VMEM((2, ACT, ACT // 2 + 1, BS, 128), BF16),
            pltpu.VMEM((ROWS, 2, BS, WIDTH), BF16),
            pltpu.VMEM((ROWS, 3, BS, WIDTH), BF16),
            pltpu.VMEM((2, BLK_DEV, BS, WIDTH), BF16),
            pltpu.VMEM((2, BLK_DEV, BS, WIDTH), BF16),
            pltpu.SMEM((3 * ROWS,), jnp.int32),
            pltpu.SMEM((ACT,), jnp.int32),
            pltpu.SMEM((ACT * ACT,), jnp.int32),
            pltpu.SMEM((ACT * KNZ,), jnp.int32),
            pltpu.SMEM((2 * ROWS,), jnp.int32),
            pltpu.SemaphoreType.DMA((2,)),
            pltpu.SemaphoreType.DMA((4,)),
            pltpu.SemaphoreType.DMA((4,)),
            pltpu.SemaphoreType.DMA((30,)),
            pltpu.SemaphoreType.DMA((30,)),
        ],
        compiler_params=pltpu.CompilerParams(
            collective_id=0, has_side_effects=True, vmem_limit_bytes=56 << 20
        ),
    )(
        active.T,
        pattern.T,
        grid_weights.reshape(1, PTS),
        basis_values,
        density_blocks.reshape(BLK_DEV, BS, WIDTH),
    )
    return dens.reshape(PTS), ham.reshape(BLK_DEV * BS, WIDTH)


def solution(mesh):
    placed = (
        P(("region", "rows"), None),
        P(("region", "rows")),
        P(("region", "rows"), None),
        P(),
        P(),
    )
    return jax.shard_map(
        shards,
        mesh=mesh,
        in_specs=placed,
        out_specs=(P(("region", "rows")), P(("region", "rows"), None)),
        check_vma=False,
    )
```

time: 198 us -> 154 us (0.78)
  Pallas kernels: 0 us -> 148 us
  waiting for transfers between devices: 113 us -> 0 us
  local copies, waits for them, and re-layouts: 38.3 us -> 3.56 us
  starting transfers between devices: 20.3 us -> 0 us
  matrix products: 17.1 us -> 0 us
  other arithmetic: 7.5 us -> 1.31 us
    pallas_call x0 -> x1, Pallas kernels: none -> 148 us  [shards(): pl.pallas_call(kernel, out_shape=(jax.ShapeDtypeStruct((1, PTS), F32), ja...]
    all_to_all x2 -> x0, waiting for transfers between devices: 92.2 us -> none  [the longest x1 50.7 us: shards(): lax.all_to_all(sending.reshape(row_count, capacity, BS, wire_width), 'row...]
    ppermute x4 -> x0, waiting for transfers between devices: 20.5 us -> none  [the longest x1 9.87 us: with_halo(): before = lax.ppermute(last, axis, up)]
    dot_general x5 -> x0, matrix products: 17.1 us -> none  [the longest x1 5.97 us: shards(): jnp.dot(basis_values, sub_density, preferred_element_type=jnp.float32)]
    all_to_all x2 -> x0, starting transfers between devices: 15.1 us -> none  [the longest x1 10.8 us: shards(): lax.all_to_all(outgoing, 'rows', split_axis=0, concat_axis=0, tiled=True)]
    reshape x5 -> x1, local copies, waits for them, and re-layouts: 15.5 us -> 1.29 us  [shards(): grid_weights.reshape(1, PTS)]
    ppermute x4 -> x0, starting transfers between devices: 5.16 us -> none  [the longest x1 2.76 us: with_halo(): before = lax.ppermute(last, axis, up)]
    convert_element_type x2 -> x0, local copies, waits for them, and re-layouts: 4.18 us -> none  [the longest x1 2.09 us: shards(): grouped[2].astype(jnp.bfloat16)]
  transfers between devices with their start and end apart: 6 -> 0, of which waited for: 5 -> 0; matrix products, arithmetic and copies ran while one was open for 6% -> 0% of each run, Pallas kernels for 0% -> 0%
where the time goes in v1:
time: 154 us
  Pallas kernels  148 us (96%)
  local copies, waits for them, and re-layouts  3.56 us (2%)
    pallas_call x1, Pallas kernels, shards(): pl.pallas_call(kernel, out_shape=(jax.ShapeDtypeStruct((1, PTS), F32), ja...  148 us

profile of v1, /device:TPU:1, one launch (start us, length us, event | category | flops | bytes accessed | tf_op | source)
XLA Modules:
  0.0 154.0 jit_solution(1692713487846762609)
XLA Ops:
  0.6 1.3 reshape.16.weights
  1.9 148.5 %shard_map.68 = (f32[1,1536]{1,0:T(1,128)}, f32[8,64,512]{2,1,0:T(8,128)}) custom-call(s32[16,256]{1,0:T(8,128)} %bitcast.7, s32[8,2048]{1,0:T(8,128)} %bitcast.6, f32[1,1536]{1,0:T(1,128)} %reshape.16.weights, bf16[1536,1024]{1,0:T(8,128)(2,1)} %x_hbm.1, bf16[8,64,512]{2,1,0:T(8,128)(2,1)} %bitcast.5), custom_call_target="tpu_custom_call" | custom-call | tf_op jit(solution)/shard_map/pallas_call | solution.py:295
  150.4 1.3 reduce
  151.7 2.3 %copy.8 = f32[512,512]{1,0:T(8,128)} copy(f32[512,512]{1,0:T(8,128)} %bitcast.4) | data formatting | bytes 2097152

commit v2 on v1

--- a/solution.py
+++ b/solution.py
@@ -16,6 +16,7 @@
 WIDTH = KNZ * BS
 COLS = ACT * BS
 CHUNK = 256
+HALO = 2
 MESH = pl.DeviceIdType.MESH
 F32 = jnp.float32
 BF16 = jnp.bfloat16
@@ -34,18 +35,27 @@
     return low, high
 
 
+def two_blocks(source, row_a, block_a, row_b, block_b, masks):
+    low, high = masks
+    a = source[block_a & 1, row_a, block_a >> 1]
+    b = source[1 - (block_b & 1), row_b, block_b >> 1]
+    return a * low + b * high
+
+
 def pair_of_blocks(source, row, first, second, masks):
-    low, high = masks
-    a = source[first & 1, row, first >> 1]
-    b = source[1 - (second & 1), row, second >> 1]
-    return a * low + b * high
+    return two_blocks(source, row, first, row, second, masks)
 
 
 def swap_halves(values):
     return pltpu.roll(values, 64, 1)
 
 
-def kernel(
+def keep_both(target, row, part, values):
+    target[0, row, part] = values
+    target[1, row, part] = swap_halves(values.astype(F32)).astype(BF16)
+
+
+def full_kernel(
     act, pat, weights, x_hbm, d_hbm,
     dens_out, ham_out,
     xv, xt, ext, send_d, recv_d, rows2, dfull, svec, hrows, send_h, recv_h,
@@ -288,17 +298,463 @@
         copy.wait_send()
 
 
-def shards(basis_values, grid_weights, density_blocks, pattern, active):
+def offset_of(i):
+    j = lax.div(i, 2)
+    dz = 4 + lax.div(j + 1, 2) * (1 - 2 * lax.rem(j, 2))
+    return 1 - lax.rem(i, 2), dz
+
+
+def packed_kernel(
+    act, pat, weights, x_hbm, d_hbm,
+    dens_out, ham_out, flag_out,
+    xv, xt, own, halo_d, ext2, send_d, recv_d, rows2, dfull, svec, hrows, send_h,
+    recv_h, hvar, expanded, halo_out, halo_in, row_flags, region_flags,
+    halo_src, row_map, back_map, tab_row, tab_src, tab_pos,
+    tab_j, tab_rank, tab_local, tab_q, tab_start, tab_owner, tab_dpos, tab_h,
+    local_sems, halo_send, halo_recv, a2a_send, a2a_recv, flag_send, flag_recv,
+):
+    g = lax.axis_index("region")
+    me = lax.axis_index("rows")
+    y = lax.div(me, 8)
+    z = lax.rem(me, 8)
+    left, right = lax.rem(g + 15, 16), lax.rem(g + 1, 16)
+
+    def peer(i):
+        dy, dz = offset_of(i)
+        return lax.rem(y + dy, 2) * 8 + lax.rem(z + dz, 8)
+
+    def sender(i):
+        dy, dz = offset_of(i)
+        return lax.rem(y + dy, 2) * 8 + lax.rem(z + 8 - dz, 8)
+
+    x_copy = pltpu.make_async_copy(x_hbm, xv, local_sems.at[0])
+    d_copy = pltpu.make_async_copy(d_hbm, own, local_sems.at[1])
+    d_copy.start()
+    x_copy.start()
+
+    barrier = pltpu.get_barrier_semaphore()
+    for n in (left, right) + tuple(lax.rem(g + 16 - hop, 16) for hop in (2, 4, 8)):
+        pl.semaphore_signal(barrier, inc=1, device_id=(n, me), device_id_type=MESH)
+
+    def greet(i, carry):
+        pl.semaphore_signal(barrier, inc=1, device_id=(g, peer(i)), device_id_type=MESH)
+        return carry
+
+    lax.fori_loop(0, ROWS - 1, greet, 0)
+
+    def named(region, start):
+        def one(b, mask):
+            for e in range(start, start + 4):
+                block = act[e, region * ROWS + b]
+                bit = (1 + (block & 1)) * (1 + 3 * ((block >> 1) & 1)) * (1 + 15 * ((block >> 2) & 1))
+                mask = mask | jnp.where(((block >> 3) & (ROWS - 1)) == me, bit, 0)
+            return mask
+
+        return lax.fori_loop(0, ROWS, one, jnp.int32(0))
+
+    def ranks(mask):
+        taken = jnp.int32(0)
+        bits, places = [], []
+        for s in range(BLK_DEV):
+            bit = (mask >> s) & 1
+            bits.append(bit)
+            places.append(taken)
+            taken = taken + bit
+        return bits, places, taken
+
+    overflow = jnp.int32(0)
+    for side, mask in enumerate((named(right, 8), named(left, 12))):
+        bits, places, taken = ranks(mask)
+        for i in range(HALO):
+            source = jnp.int32(0)
+            for s in range(BLK_DEV):
+                source = jnp.where((bits[s] == 1) & (places[s] == i), s, source)
+            halo_src[side * HALO + i] = source
+        for s in range(BLK_DEV):
+            back_map[side * BLK_DEV + s] = jnp.where(bits[s] == 1, jnp.minimum(places[s], HALO - 1), HALO)
+        overflow = jnp.maximum(overflow, (taken > HALO).astype(jnp.int32))
+
+    d_copy.wait()
+    for side in range(2):
+        for i in range(HALO):
+            halo_out[side, i] = own[halo_src[side * HALO + i]]
+    pl.semaphore_wait(barrier, 20)
+
+    to_right = pltpu.make_async_remote_copy(
+        halo_out.at[0], halo_d.at[0], halo_send.at[0], halo_recv.at[0],
+        device_id=(right, me), device_id_type=MESH)
+    to_left = pltpu.make_async_remote_copy(
+        halo_out.at[1], halo_d.at[1], halo_send.at[1], halo_recv.at[1],
+        device_id=(left, me), device_id_type=MESH)
+    to_right.start()
+    to_left.start()
+
+    for side, start in ((0, 8), (1, 12)):
+        bits, places, taken = ranks(named(g, start))
+        for s in range(BLK_DEV):
+            row_map[2 * side * BLK_DEV + s] = side * (HALO + BLK_DEV) + jnp.minimum(places[s], HALO - 1)
+    for s in range(BLK_DEV):
+        row_map[BLK_DEV + s] = HALO + s
+
+    def own_row_twice(s, carry):
+        for q in range(KNZ // 2):
+            keep_both(ext2, HALO + s, q, own[s, :, q * 128 : (q + 1) * 128])
+        return carry
+
+    lax.fori_loop(0, BLK_DEV, own_row_twice, 0)
+
+    def batch_table(b):
+        ids = [act[e, g * ROWS + b] for e in range(ACT)]
+        blocks = [jnp.int32(0), jnp.int32(0)]
+        count = jnp.int32(0)
+        for e in range(ACT):
+            mine = ((ids[e] >> 3) & (ROWS - 1)) == me
+            blocks[0] = jnp.where(mine & (count == 0), ids[e], blocks[0])
+            blocks[1] = jnp.where(mine & (count == 1), ids[e], blocks[1])
+            count = count + mine.astype(jnp.int32)
+        packed = [jnp.int32(0)] * KNZ
+        running = jnp.int32(0)
+        for c in range(2):
+            group = jnp.minimum(((blocks[c] >> 7) - g + 1) & 15, 2)
+            tab_row[2 * b + c] = row_map[group * BLK_DEV + (blocks[c] & 7)]
+            valid = count > c
+            for m in range(KNZ):
+                column = pat[m, blocks[c]]
+                gap = column ^ ids[0]
+                for e in range(1, ACT):
+                    gap = jnp.minimum(gap, column ^ ids[e])
+                match = (gap == 0) & valid
+                for p in range(m + 1 if c == 0 else KNZ):
+                    packed[p] = jnp.where(match & (running == p), c * KNZ + m, packed[p])
+                tab_pos[b * 16 + c * KNZ + m] = jnp.where(match, jnp.minimum(running, KNZ - 1), KNZ)
+                running = running + match.astype(jnp.int32)
+        for p in range(KNZ):
+            tab_src[b * KNZ + p] = packed[p]
+        tab_row[2 * ROWS + b] = count
+
+    masks = half_masks()
+
+    def pack_rows(b, target):
+        for q in range(KNZ // 2):
+            a = tab_src[b * KNZ + 2 * q]
+            c = tab_src[b * KNZ + 2 * q + 1]
+            target[b if target is send_d else me, q] = two_blocks(
+                ext2, tab_row[2 * b + (a >> 3)], a & 7, tab_row[2 * b + (c >> 3)], c & 7, masks)
+
+    def first_copy(i):
+        p = peer(i)
+        return pltpu.make_async_remote_copy(
+            send_d.at[p], recv_d.at[me], a2a_send.at[i], a2a_recv.at[i],
+            device_id=(g, p), device_id_type=MESH)
+
+    batch_table(peer(0))
+    to_right.wait_recv()
+    to_left.wait_recv()
+    for side in range(2):
+        for i in range(HALO):
+            for q in range(KNZ // 2):
+                keep_both(ext2, side * (HALO + BLK_DEV) + i, q, halo_d[side, i, :, q * 128 : (q + 1) * 128])
+
+    def send_first(i, carry):
+        pack_rows(peer(i), send_d)
+        first_copy(i).start()
+        following = peer(i + 1)
+        batch_table(following)
+        return carry
+
+    lax.fori_loop(0, ROWS - 1, send_first, 0)
+    pack_rows(me, recv_d)
+
+    def match_row(k, carry):
+        block = act[k, g * ROWS + me]
+        tab_owner[k] = (block >> 3) & (ROWS - 1)
+        local = [jnp.int32(KNZ)] * ACT
+        running = jnp.int32(0)
+        for m in range(KNZ):
+            column = pat[m, block]
+            found = jnp.int32(ACT)
+            for j in range(ACT):
+                same = column == act[j, g * ROWS + me]
+                found = jnp.where(same, j, found)
+                local[j] = jnp.where(same, running, local[j])
+            tab_j[k * KNZ + m] = found
+            tab_rank[k * KNZ + m] = jnp.where(found < ACT, running, 64)
+            running = running + (found < ACT).astype(jnp.int32)
+        for j in range(ACT):
+            tab_local[k * ACT + j] = local[j]
+        tab_q[k] = running
+        return carry
+
+    lax.fori_loop(0, ACT, match_row, 0)
+
+    def start_row(k, most):
+        start = jnp.int32(0)
+        for j in range(ACT):
+            start = start + jnp.where((j < k) & (tab_owner[j] == tab_owner[k]), tab_q[j], 0)
+        tab_start[k] = start
+        for j in range(ACT):
+            local = tab_local[k * ACT + j]
+            tab_dpos[k * ACT + j] = jnp.where(local < KNZ, jnp.minimum(start + local, KNZ - 1), KNZ)
+        return jnp.maximum(most, start + tab_q[k])
+
+    most = lax.fori_loop(0, ACT, start_row, jnp.int32(0))
+    overflow = jnp.maximum(overflow, (most > KNZ).astype(jnp.int32))
+
+    row_flags[me] = jnp.full((8, 128), overflow, jnp.int32)
+
+    def row_flag_copy(i):
+        p = peer(i)
+        return pltpu.make_async_remote_copy(
+            row_flags.at[me], row_flags.at[me], flag_send.at[i], flag_recv.at[i],
+            device_id=(g, p), device_id_type=MESH)
+
+    def region_flag_copy(r):
+        return pltpu.make_async_remote_copy(
+            region_flags.at[0, r], region_flags.at[1, r], flag_send.at[15 + r], flag_recv.at[15 + r],
+            device_id=(lax.rem(g + 2**r, 16), me), device_id_type=MESH)
+
+    def merge_flags(r):
+        region_flag_copy(r).wait_recv()
+        merged = jnp.maximum(region_flags[0, r], region_flags[1, r])
+        if r < 3:
+            region_flags[0, r + 1] = merged
+            region_flag_copy(r + 1).start()
+        else:
+            flag_out[...] = merged
+
+    def send_flag(i, carry):
+        row_flag_copy(i).start()
+        return carry
+
+    lax.fori_loop(0, ROWS - 1, send_flag, 0)
+
+    def slot_table(r, carry):
+        entries = [jnp.int32(0), jnp.int32(0)]
+        count = jnp.int32(0)
+        for k in range(ACT):
+            mine = tab_owner[k] == r
+            entries[0] = jnp.where(mine & (count == 0), k, entries[0])
+            entries[1] = jnp.where(mine & (count == 1), k, entries[1])
+            count = count + mine.astype(jnp.int32)
+        packed = [jnp.int32(0)] * KNZ
+        for c in range(2):
+            k = entries[c]
+            start = jnp.where(count > c, tab_start[k], 64)
+            for m in range(KNZ):
+                place = start + tab_rank[k * KNZ + m]
+                code = k * ACT + jnp.minimum(tab_j[k * KNZ + m], ACT - 1)
+                for p in range(m + 1 if c == 0 else KNZ):
+                    packed[p] = jnp.where(place == p, code, packed[p])
+        for p in range(KNZ):
+            tab_h[r * KNZ + p] = packed[p]
+        return carry
+
+    lax.fori_loop(0, ROWS, slot_table, 0)
+
+    rows2[:, :, KNZ // 2] = jnp.zeros((2, ROWS, BS, 128), BF16)
+    hvar[:, :, KNZ // 2] = jnp.zeros((2, ROWS, BS, 128), BF16)
+    expanded[2 * ROWS] = jnp.zeros((KNZ // 2, BS, 128), BF16)
+    for side in range(2):
+        halo_in[side, HALO] = jnp.zeros((BS, WIDTH), BF16)
+
+    x_copy.wait()
+
+    def transpose_chunk(i, carry):
+        points = pl.ds(pl.multiple_of(i * 128, 128), 128)
+        xt[:, points] = jnp.transpose(xv[points, :])
+        return carry
+
+    lax.fori_loop(0, PTS // 128, transpose_chunk, 0)
+
+    def spread_slot(r):
+        for q in range(KNZ // 2):
+            keep_both(rows2, r, q, recv_d[r, q])
+
+    spread_slot(me)
+
+    def take_first(i, carry):
+        first_copy(i).wait_recv()
+        spread_slot(sender(i))
+        return carry
+
+    lax.fori_loop(0, ROWS - 1, take_first, 0)
+
+    def assemble_row(k, carry):
+        owner = tab_owner[k]
+        for q in range(ACT // 2):
+            dfull[pl.ds(pl.multiple_of(k * BS, BS), BS), q * 128 : (q + 1) * 128] = pair_of_blocks(
+                rows2, owner, tab_dpos[k * ACT + 2 * q], tab_dpos[k * ACT + 2 * q + 1], masks)
+        return carry
+
+    lax.fori_loop(0, ACT, assemble_row, 0)
+
+    def density_chunk(i, carry):
+        points = pl.ds(pl.multiple_of(i * CHUNK, CHUNK), CHUNK)
+        x = xv[points, :]
+        part = jnp.zeros((CHUNK, 128), F32)
+        for n in range(COLS // CHUNK):
+            product = jnp.dot(x, dfull[:, n * CHUNK : (n + 1) * CHUNK], preferred_element_type=F32)
+            product = product * x[:, n * CHUNK : (n + 1) * CHUNK].astype(F32)
+            part = part + (product[:, :128] + product[:, 128:])
+        dens = jnp.sum(jnp.transpose(part), axis=0, keepdims=True)
+        dens_out[:, points] = dens
+        svec[:, points] = weights[:, points] * jnp.tanh(dens)
+        return carry
+
+    lax.fori_loop(0, PTS // CHUNK, density_chunk, 0)
+
+    def take_flag(i, carry):
+        row_flag_copy(i).wait_recv()
+        return carry
+
+    lax.fori_loop(0, ROWS - 1, take_flag, 0)
+    merged = row_flags[0]
+    for r in range(1, ROWS):
+        merged = jnp.maximum(merged, row_flags[r])
+    region_flags[0, 0] = merged
+    region_flag_copy(0).start()
+
+    def ham_chunk(i, carry):
+        scaled = (xt[pl.ds(pl.multiple_of(i * CHUNK, CHUNK), CHUNK), :].astype(F32) * svec[...]).astype(BF16)
+        for n in range(COLS // CHUNK):
+            block = jnp.dot(scaled, xv[:, n * CHUNK : (n + 1) * CHUNK], preferred_element_type=F32)
+            for half in range(CHUNK // 128):
+                part = block[:, half * 128 : (half + 1) * 128]
+                swapped = swap_halves(part).astype(BF16)
+                part = part.astype(BF16)
+                for kk in range(CHUNK // BS):
+                    entry = i * (CHUNK // BS) + kk
+                    hrows[0, entry, 2 * n + half] = part[kk * BS : (kk + 1) * BS]
+                    hrows[1, entry, 2 * n + half] = swapped[kk * BS : (kk + 1) * BS]
+        return carry
+
+    lax.fori_loop(0, COLS // CHUNK, ham_chunk, 0)
+
+    def pack_slot(r, target, target_row):
+        for q in range(KNZ // 2):
+            a = tab_h[r * KNZ + 2 * q]
+            b = tab_h[r * KNZ + 2 * q + 1]
+            target[target_row, q] = two_blocks(hrows, a >> 4, a & 15, b >> 4, b & 15, masks)
+
+    def second_copy(i):
+        p = peer(i)
+        return pltpu.make_async_remote_copy(
+            send_h.at[p], recv_h.at[me], a2a_send.at[15 + i], a2a_recv.at[15 + i],
+            device_id=(g, p), device_id_type=MESH)
+
+    def send_second(i, carry):
+        p = peer(i)
+        pack_slot(p, send_h, p)
+        second_copy(i).start()
+        return carry
+
+    lax.fori_loop(0, ROWS - 1, send_second, 0)
+    pack_slot(me, recv_h, me)
+
+    merge_flags(0)
+    merge_flags(1)
+    merge_flags(2)
+
+    def expand_slot(b):
+        for q in range(KNZ // 2):
+            keep_both(hvar, b, q, recv_h[b, q])
+        for c in range(2):
+            for q in range(KNZ // 2):
+                expanded[2 * b + c, q] = pair_of_blocks(
+                    hvar, b, tab_pos[b * 16 + c * KNZ + 2 * q], tab_pos[b * 16 + c * KNZ + 2 * q + 1], masks)
+
+    expand_slot(me)
+
+    def take_second(i, carry):
+        second_copy(i).wait_recv()
+        expand_slot(sender(i))
+        return carry
+
+    lax.fori_loop(0, ROWS - 1, take_second, 0)
+
+    def sum_row(t):
+        picks = []
+        for b in range(ROWS):
+            count = tab_row[2 * ROWS + b]
+            picks.append(jnp.where(
+                (tab_row[2 * b] == t) & (count > 0), 2 * b,
+                jnp.where((tab_row[2 * b + 1] == t) & (count > 1), 2 * b + 1, 2 * ROWS)))
+        total = expanded[picks[0]].astype(F32)
+        for b in range(1, ROWS):
+            total = total + expanded[picks[b]].astype(F32)
+        return total
+
+    to_right.wait_send()
+    to_left.wait_send()
+
+    def side_row(t, carry):
+        for side in range(2):
+            total = sum_row(side * (HALO + BLK_DEV) + t).astype(BF16)
+            for q in range(KNZ // 2):
+                halo_out[side, t, :, q * 128 : (q + 1) * 128] = total[q]
+        return carry
+
+    lax.fori_loop(0, HALO, side_row, 0)
+
+    back_left = pltpu.make_async_remote_copy(
+        halo_out.at[0], halo_in.at[0, pl.ds(0, HALO)], halo_send.at[2], halo_recv.at[2],
+        device_id=(left, me), device_id_type=MESH)
+    back_right = pltpu.make_async_remote_copy(
+        halo_out.at[1], halo_in.at[1, pl.ds(0, HALO)], halo_send.at[3], halo_recv.at[3],
+        device_id=(right, me), device_id_type=MESH)
+    back_left.start()
+    back_right.start()
+
+    def own_row(t, carry):
+        total = sum_row(HALO + t)
+        for q in range(KNZ // 2):
+            ham_out[t, :, q * 128 : (q + 1) * 128] = total[q]
+        return carry
+
+    lax.fori_loop(0, BLK_DEV, own_row, 0)
+    merge_flags(3)
+    back_left.wait_recv()
+    back_right.wait_recv()
+
+    def add_row(t, carry):
+        ham_out[t] = (
+            ham_out[t]
+            + halo_in[0, back_map[t]].astype(F32)
+            + halo_in[1, back_map[BLK_DEV + t]].astype(F32)
+        )
+        return carry
+
+    lax.fori_loop(0, BLK_DEV, add_row, 0)
+
+    def finish(i, carry):
+        first_copy(i).wait_send()
+        second_copy(i).wait_send()
+        row_flag_copy(i).wait_send()
+        return carry
+
+    lax.fori_loop(0, ROWS - 1, finish, 0)
+    for r in range(4):
+        region_flag_copy(r).wait_send()
+    back_left.wait_send()
+    back_right.wait_send()
+
+
+def specs():
     vmem = pl.BlockSpec(memory_space=pltpu.VMEM)
     smem = pl.BlockSpec(memory_space=pltpu.SMEM)
     hbm = pl.BlockSpec(memory_space=pl.ANY)
-    dens, ham = pl.pallas_call(
-        kernel,
+    return [smem, smem, vmem, hbm, hbm], vmem
+
+
+def full_capacity(act, pat, weights, x, d):
+    in_specs, vmem = specs()
+    return pl.pallas_call(
+        full_kernel,
         out_shape=(
             jax.ShapeDtypeStruct((1, PTS), F32),
             jax.ShapeDtypeStruct((BLK_DEV, BS, WIDTH), F32),
         ),
-        in_specs=[smem, smem, vmem, hbm, hbm],
+        in_specs=in_specs,
         out_specs=(vmem, vmem),
         scratch_shapes=[
             pltpu.VMEM((PTS, COLS), BF16),
@@ -326,15 +782,81 @@
             pltpu.SemaphoreType.DMA((30,)),
         ],
         compiler_params=pltpu.CompilerParams(
+            collective_id=1, has_side_effects=True, vmem_limit_bytes=56 << 20
+        ),
+    )(act, pat, weights, x, d)
+
+
+def packed_capacity(act, pat, weights, x, d):
+    in_specs, vmem = specs()
+    half = KNZ // 2
+    return pl.pallas_call(
+        packed_kernel,
+        out_shape=(
+            jax.ShapeDtypeStruct((1, PTS), F32),
+            jax.ShapeDtypeStruct((BLK_DEV, BS, WIDTH), F32),
+            jax.ShapeDtypeStruct((8, 128), jnp.int32),
+        ),
+        in_specs=in_specs,
+        out_specs=(vmem, vmem, vmem),
+        scratch_shapes=[
+            pltpu.VMEM((PTS, COLS), BF16),
+            pltpu.VMEM((COLS, PTS), BF16),
+            pltpu.VMEM((BLK_DEV, BS, WIDTH), BF16),
+            pltpu.VMEM((2, HALO, BS, WIDTH), BF16),
+            pltpu.VMEM((2, BLK_DEV + 2 * HALO, half, BS, 128), BF16),
+            pltpu.VMEM((ROWS, half, BS, 128), BF16),
+            pltpu.VMEM((ROWS, half, BS, 128), BF16),
+            pltpu.VMEM((2, ROWS, half + 1, BS, 128), BF16),
+            pltpu.VMEM((COLS, COLS), BF16),
+            pltpu.VMEM((1, PTS), F32),
+            pltpu.VMEM((2, ACT, ACT // 2, BS, 128), BF16),
+            pltpu.VMEM((ROWS, half, BS, 128), BF16),
+            pltpu.VMEM((ROWS, half, BS, 128), BF16),
+            pltpu.VMEM((2, ROWS, half + 1, BS, 128), BF16),
+            pltpu.VMEM((2 * ROWS + 1, half, BS, 128), BF16),
+            pltpu.VMEM((2, HALO, BS, WIDTH), BF16),
+            pltpu.VMEM((2, HALO + 1, BS, WIDTH), BF16),
+            pltpu.VMEM((ROWS, 8, 128), jnp.int32),
+            pltpu.VMEM((2, 4, 8, 128), jnp.int32),
+            pltpu.SMEM((2 * HALO,), jnp.int32),
+            pltpu.SMEM((3 * BLK_DEV,), jnp.int32),
+            pltpu.SMEM((2 * BLK_DEV,), jnp.int32),
+            pltpu.SMEM((3 * ROWS,), jnp.int32),
+            pltpu.SMEM((ROWS * KNZ,), jnp.int32),
+            pltpu.SMEM((ROWS * 2 * KNZ,), jnp.int32),
+            pltpu.SMEM((ACT * KNZ,), jnp.int32),
+            pltpu.SMEM((ACT * KNZ,), jnp.int32),
+            pltpu.SMEM((ACT * ACT,), jnp.int32),
+            pltpu.SMEM((ACT,), jnp.int32),
+            pltpu.SMEM((ACT,), jnp.int32),
+            pltpu.SMEM((ACT,), jnp.int32),
+            pltpu.SMEM((ACT * ACT,), jnp.int32),
+            pltpu.SMEM((ROWS * KNZ,), jnp.int32),
+            pltpu.SemaphoreType.DMA((2,)),
+            pltpu.SemaphoreType.DMA((4,)),
+            pltpu.SemaphoreType.DMA((4,)),
+            pltpu.SemaphoreType.DMA((30,)),
+            pltpu.SemaphoreType.DMA((30,)),
+            pltpu.SemaphoreType.DMA((19,)),
+            pltpu.SemaphoreType.DMA((19,)),
+        ],
+        compiler_params=pltpu.CompilerParams(
             collective_id=0, has_side_effects=True, vmem_limit_bytes=56 << 20
         ),
-    )(
+    )(act, pat, weights, x, d)
+
+
+def shards(basis_values, grid_weights, density_blocks, pattern, active):
+    args = (
         active.T,
         pattern.T,
         grid_weights.reshape(1, PTS),
         basis_values,
         density_blocks.reshape(BLK_DEV, BS, WIDTH),
     )
+    dens, ham, flag = packed_capacity(*args)
+    dens, ham = lax.cond(flag[0, 0] > 0, lambda: tuple(full_capacity(*args)), lambda: (dens, ham))
     return dens.reshape(PTS), ham.reshape(BLK_DEV * BS, WIDTH)
 
 

time: 154 us -> 90.4 us (0.59)
  Pallas kernels: 148 us -> 85.5 us
    pallas_call x1, Pallas kernels: 148 us -> 85.5 us  [packed_capacity(): pl.pallas_call(packed_kernel, out_shape=(jax.ShapeDtypeStruct((1, PTS), F...]
where the time goes in v2:
time: 90.4 us; the launch traced here: 90 us
  Pallas kernels  85.5 us (95%)
  local copies, waits for them, and re-layouts  3.05 us (3%)
  between operations  1.37 us (2%)
    pallas_call x1, Pallas kernels, packed_capacity(): pl.pallas_call(packed_kernel, out_shape=(jax.ShapeDtypeStruct((1, PTS), F...  85.5 us

profile of v2, /device:TPU:1, one launch (start us, length us, event | category | flops | bytes accessed | tf_op | source)
XLA Modules:
  0.0 90.0 jit_solution(7243149336327747609)
XLA Ops:
  0.6 0.0 copy-start
  0.6 0.0 copy-start.3
  0.7 0.0 copy-start.2
  0.7 0.0 copy-start.1
  0.7 0.9 reshape.28.weights
  1.5 85.5 %shard_map.68 = (f32[1,1536]{1,0:T(1,128)S(1)}, f32[8,64,512]{2,1,0:T(8,128)S(1)}, s32[8,128]{1,0:T(8,128)}) custom-call(s32[16,256]{1,0:T(8,128)} %bitcast.12, s32[8,2048]{1,0:T(8,128)} %bitcast.10, f32[1,1536]{1,0:T(1,128)S(1)} %reshape.28.weights, bf16[1536,1024]{1,0:T(8,128)(2,1)} %x_hbm.1, bf16[8,64,512]{2,1,0:T(8,128)(2,1)} %bitcast.6), custom_call_target="tpu_custom_call" | custom-call | tf_op jit(solution)/shard_map/pallas_call | solution.py:793
  87.1 1.2 %slice.3 = s32[1,1]{1,0:T(1,128)} slice(s32[8,128]{1,0:T(8,128)} %get-tuple-element.34), slice={[0:1], [0:1]} | slice | bytes 8 | tf_op jit(solution)/shard_map/slice | solution.py:859
  88.9 0.0 copy-done
  88.9 0.0 copy-done.3
  88.9 0.0 copy-done.2
  88.9 0.0 copy-done.1
  89.0 0.0 copy-start.4
  89.0 1.0 %copy.13 = f32[512,512]{1,0:T(8,128)} copy(f32[512,512]{1,0:T(8,128)S(1)} %get-tuple-element.54) | data formatting | bytes 2097152
  90.0 0.0 copy-done.4
  (2 shorter events, 0.1 us)
Async XLA Ops:
  0.6 88.3 %copy-start = (bf16[1536,1024]{1,0:T(8,128)(2,1)S(1)}, bf16[1536,1024]{1,0:T(8,128)(2,1)}, u32[]{:S(2)}) copy-start(bf16[1536,1024]{1,0:T(8,128)(2,1)} %x_hbm.1) | copy-start | bytes 9437188
  0.6 88.3 %copy-start.3 = (s32[256,16]{0,1:T(8,128)S(1)}, s32[256,16]{0,1:T(8,128)}, u32[]{:S(2)}) copy-start(s32[256,16]{0,1:T(8,128)} %param.11) | copy-start | bytes 49156
  0.7 88.3 %copy-start.2 = (s32[2048,8]{0,1:T(8,128)S(1)}, s32[2048,8]{0,1:T(8,128)}, u32[]{:S(2)}) copy-start(s32[2048,8]{0,1:T(8,128)} %param.10) | copy-start | bytes 196612
  0.7 88.3 %copy-start.1 = (bf16[512,512]{1,0:T(8,128)(2,1)S(1)}, bf16[512,512]{1,0:T(8,128)(2,1)}, u32[]{:S(2)}) copy-start(bf16[512,512]{1,0:T(8,128)(2,1)} %param.9) | copy-start | bytes 1572868
  89.0 1.0 %copy-start.4 = (f32[1536]{0:T(1024)}, f32[1536]{0:T(1024)S(1)}, u32[]{:S(2)}) copy-start(f32[1536]{0:T(1024)S(1)} %get-tuple-element.53) | copy-start | bytes 18436

commit v3 on v2

--- a/solution.py
+++ b/solution.py
@@ -16,7 +16,7 @@
 WIDTH = KNZ * BS
 COLS = ACT * BS
 CHUNK = 256
-HALO = 2
+HALO = 1
 MESH = pl.DeviceIdType.MESH
 F32 = jnp.float32
 BF16 = jnp.bfloat16
@@ -203,8 +203,11 @@
             product = product * x[:, n * CHUNK : (n + 1) * CHUNK].astype(F32)
             part = part + (product[:, :128] + product[:, 128:])
         dens = jnp.sum(jnp.transpose(part), axis=0, keepdims=True)
-        dens_out[:, points] = dens
-        svec[:, points] = weights[:, points] * jnp.tanh(dens)
+        for half in range(CHUNK // 128):
+            row = pl.ds(i * (CHUNK // 128) + half, 1)
+            dens_half = dens[:, half * 128 : (half + 1) * 128]
+            dens_out[row, :] = dens_half
+            svec[:, pl.ds(pl.multiple_of(i * CHUNK + half * 128, 128), 128)] = weights[row, :] * jnp.tanh(dens_half)
         return carry
 
     lax.fori_loop(0, PTS // CHUNK, density_chunk, 0)
@@ -310,7 +313,7 @@
     xv, xt, own, halo_d, ext2, send_d, recv_d, rows2, dfull, svec, hrows, send_h,
     recv_h, hvar, expanded, halo_out, halo_in, row_flags, region_flags,
     halo_src, row_map, back_map, tab_row, tab_src, tab_pos,
-    tab_j, tab_rank, tab_local, tab_q, tab_start, tab_owner, tab_dpos, tab_h,
+    tab_j, tab_rank, tab_local, tab_q, tab_start, tab_owner, tab_dpos, tab_h, tab_turn, tab_place, tab_order,
     local_sems, halo_send, halo_recv, a2a_send, a2a_recv, flag_send, flag_recv,
 ):
     g = lax.axis_index("region")
@@ -520,13 +523,39 @@
             region_flags[0, r + 1] = merged
             region_flag_copy(r + 1).start()
         else:
-            flag_out[...] = merged
+            flag_out[0, 0] = merged[0, 0]
 
     def send_flag(i, carry):
         row_flag_copy(i).start()
         return carry
 
     lax.fori_loop(0, ROWS - 1, send_flag, 0)
+
+    def turn_of(i, carry):
+        tab_turn[peer(i)] = i
+        return carry
+
+    lax.fori_loop(0, ROWS, turn_of, 0)
+
+    def place_of(k, carry):
+        turn = tab_turn[tab_owner[k]]
+        place = jnp.int32(0)
+        for j in range(ACT):
+            other = tab_turn[tab_owner[j]]
+            place = place + ((other < turn) | ((other == turn) & (j < k))).astype(jnp.int32)
+        tab_place[k] = place
+        return carry
+
+    lax.fori_loop(0, ACT, place_of, 0)
+
+    def entry_at(n, carry):
+        entry = jnp.int32(0)
+        for k in range(ACT):
+            entry = jnp.where(tab_place[k] == n, k, entry)
+        tab_order[n] = entry
+        return carry
+
+    lax.fori_loop(0, ACT, entry_at, 0)
 
     def slot_table(r, carry):
         entries = [jnp.int32(0), jnp.int32(0)]
@@ -542,7 +571,7 @@
             start = jnp.where(count > c, tab_start[k], 64)
             for m in range(KNZ):
                 place = start + tab_rank[k * KNZ + m]
-                code = k * ACT + jnp.minimum(tab_j[k * KNZ + m], ACT - 1)
+                code = tab_place[k] * ACT + jnp.minimum(tab_j[k * KNZ + m], ACT - 1)
                 for p in range(m + 1 if c == 0 else KNZ):
                     packed[p] = jnp.where(place == p, code, packed[p])
         for p in range(KNZ):
@@ -561,7 +590,7 @@
 
     def transpose_chunk(i, carry):
         points = pl.ds(pl.multiple_of(i * 128, 128), 128)
-        xt[:, points] = jnp.transpose(xv[points, :])
+        xt[:, :, points] = jnp.transpose(xv[points, :]).reshape(ACT, BS, 128)
         return carry
 
     lax.fori_loop(0, PTS // 128, transpose_chunk, 0)
@@ -597,8 +626,11 @@
             product = product * x[:, n * CHUNK : (n + 1) * CHUNK].astype(F32)
             part = part + (product[:, :128] + product[:, 128:])
         dens = jnp.sum(jnp.transpose(part), axis=0, keepdims=True)
-        dens_out[:, points] = dens
-        svec[:, points] = weights[:, points] * jnp.tanh(dens)
+        for half in range(CHUNK // 128):
+            row = pl.ds(i * (CHUNK // 128) + half, 1)
+            dens_half = dens[:, half * 128 : (half + 1) * 128]
+            dens_out[row, :] = dens_half
+            svec[:, pl.ds(pl.multiple_of(i * CHUNK + half * 128, 128), 128)] = weights[row, :] * jnp.tanh(dens_half)
         return carry
 
     lax.fori_loop(0, PTS // CHUNK, density_chunk, 0)
@@ -614,8 +646,27 @@
     region_flags[0, 0] = merged
     region_flag_copy(0).start()
 
+    def pack_slot(r, target, target_row):
+        for q in range(KNZ // 2):
+            a = tab_h[r * KNZ + 2 * q]
+            b = tab_h[r * KNZ + 2 * q + 1]
+            target[target_row, q] = two_blocks(hrows, a >> 4, a & 15, b >> 4, b & 15, masks)
+
+    def second_copy(i):
+        p = peer(i)
+        return pltpu.make_async_remote_copy(
+            send_h.at[p], recv_h.at[me], a2a_send.at[15 + i], a2a_recv.at[15 + i],
+            device_id=(g, p), device_id_type=MESH)
+
+    def send_second(i, carry):
+        p = peer(i)
+        pack_slot(p, send_h, p)
+        second_copy(i).start()
+        return carry
+
     def ham_chunk(i, carry):
-        scaled = (xt[pl.ds(pl.multiple_of(i * CHUNK, CHUNK), CHUNK), :].astype(F32) * svec[...]).astype(BF16)
+        rows = [xt[tab_order[i * (CHUNK // BS) + n]] for n in range(CHUNK // BS)]
+        scaled = (jnp.concatenate(rows, axis=0).astype(F32) * svec[...]).astype(BF16)
         for n in range(COLS // CHUNK):
             block = jnp.dot(scaled, xv[:, n * CHUNK : (n + 1) * CHUNK], preferred_element_type=F32)
             for half in range(CHUNK // 128):
@@ -626,29 +677,12 @@
                     entry = i * (CHUNK // BS) + kk
                     hrows[0, entry, 2 * n + half] = part[kk * BS : (kk + 1) * BS]
                     hrows[1, entry, 2 * n + half] = swapped[kk * BS : (kk + 1) * BS]
+        send_second(2 * i, 0)
+        send_second(2 * i + 1, 0)
         return carry
 
     lax.fori_loop(0, COLS // CHUNK, ham_chunk, 0)
-
-    def pack_slot(r, target, target_row):
-        for q in range(KNZ // 2):
-            a = tab_h[r * KNZ + 2 * q]
-            b = tab_h[r * KNZ + 2 * q + 1]
-            target[target_row, q] = two_blocks(hrows, a >> 4, a & 15, b >> 4, b & 15, masks)
-
-    def second_copy(i):
-        p = peer(i)
-        return pltpu.make_async_remote_copy(
-            send_h.at[p], recv_h.at[me], a2a_send.at[15 + i], a2a_recv.at[15 + i],
-            device_id=(g, p), device_id_type=MESH)
-
-    def send_second(i, carry):
-        p = peer(i)
-        pack_slot(p, send_h, p)
-        second_copy(i).start()
-        return carry
-
-    lax.fori_loop(0, ROWS - 1, send_second, 0)
+    lax.fori_loop(2 * (COLS // CHUNK), ROWS - 1, send_second, 0)
     pack_slot(me, recv_h, me)
 
     merge_flags(0)
@@ -751,7 +785,7 @@
     return pl.pallas_call(
         full_kernel,
         out_shape=(
-            jax.ShapeDtypeStruct((1, PTS), F32),
+            jax.ShapeDtypeStruct((PTS // 128, 128), F32),
             jax.ShapeDtypeStruct((BLK_DEV, BS, WIDTH), F32),
         ),
         in_specs=in_specs,
@@ -793,15 +827,15 @@
     return pl.pallas_call(
         packed_kernel,
         out_shape=(
-            jax.ShapeDtypeStruct((1, PTS), F32),
+            jax.ShapeDtypeStruct((PTS // 128, 128), F32),
             jax.ShapeDtypeStruct((BLK_DEV, BS, WIDTH), F32),
-            jax.ShapeDtypeStruct((8, 128), jnp.int32),
+            jax.ShapeDtypeStruct((1, 1), jnp.int32),
         ),
         in_specs=in_specs,
-        out_specs=(vmem, vmem, vmem),
+        out_specs=(vmem, vmem, in_specs[0]),
         scratch_shapes=[
             pltpu.VMEM((PTS, COLS), BF16),
-            pltpu.VMEM((COLS, PTS), BF16),
+            pltpu.VMEM((ACT, BS, PTS), BF16),
             pltpu.VMEM((BLK_DEV, BS, WIDTH), BF16),
             pltpu.VMEM((2, HALO, BS, WIDTH), BF16),
             pltpu.VMEM((2, BLK_DEV + 2 * HALO, half, BS, 128), BF16),
@@ -833,6 +867,9 @@
             pltpu.SMEM((ACT,), jnp.int32),
             pltpu.SMEM((ACT * ACT,), jnp.int32),
             pltpu.SMEM((ROWS * KNZ,), jnp.int32),
+            pltpu.SMEM((ROWS,), jnp.int32),
+            pltpu.SMEM((ACT,), jnp.int32),
+            pltpu.SMEM((ACT,), jnp.int32),
             pltpu.SemaphoreType.DMA((2,)),
             pltpu.SemaphoreType.DMA((4,)),
             pltpu.SemaphoreType.DMA((4,)),
@@ -851,7 +888,7 @@
     args = (
         active.T,
         pattern.T,
-        grid_weights.reshape(1, PTS),
+        grid_weights.reshape(PTS // 128, 128),
         basis_values,
         density_blocks.reshape(BLK_DEV, BS, WIDTH),
     )

time: 90.4 us -> 83.3 us (0.921)
  Pallas kernels: 85.5 us -> 79.9 us
  local copies, waits for them, and re-layouts: 3.05 us -> 1.59 us
    pallas_call x1, Pallas kernels: 85.5 us -> 79.9 us  [packed_capacity(): pl.pallas_call(packed_kernel, out_shape=(jax.ShapeDtypeStruct((PTS // 128...]
    slice x1 -> x0, local copies, waits for them, and re-layouts: 1.19 us -> none  [shards(): flag[0, 0] > 0]
where the time goes in v3:
time: 83.3 us; the launch traced here: 82.9 us
  Pallas kernels  79.9 us (96%)
  local copies, waits for them, and re-layouts  1.59 us (2%)
  between operations  1.35 us (2%)
    pallas_call x1, Pallas kernels, packed_capacity(): pl.pallas_call(packed_kernel, out_shape=(jax.ShapeDtypeStruct((PTS // 128...  79.9 us

profile of v3, /device:TPU:1, one launch (start us, length us, event | category | flops | bytes accessed | tf_op | source)
XLA Modules:
  0.0 82.9 jit_solution(9718283331443625316)
XLA Ops:
  0.6 0.0 copy-start
  0.6 0.0 copy-start.3
  0.7 0.0 copy-start.2
  0.7 0.0 copy-start.1
  0.7 0.0 copy-start.4
  0.7 79.9 %shard_map.68 = (f32[12,128]{1,0:T(8,128)S(1)}, f32[8,64,512]{2,1,0:T(8,128)S(1)}, s32[1,1]{1,0:T(1,128)}) custom-call(s32[16,256]{1,0:T(8,128)} %bitcast.15, s32[8,2048]{1,0:T(8,128)} %bitcast.13, f32[12,128]{1,0:T(8,128)} %bitcast.17, bf16[1536,1024]{1,0:T(8,128)(2,1)} %x_hbm.1, bf16[8,64,512]{2,1,0:T(8,128)(2,1)} %bitcast.9), custom_call_target="tpu_custom_call" | custom-call | tf_op jit(solution)/shard_map/pallas_call | solution.py:827
  81.3 0.0 copy-done
  81.3 0.0 copy-done.3
  81.3 0.0 copy-done.2
  81.3 0.0 copy-done.1
  81.3 0.0 copy-done.4
  81.3 0.6 copy.15
  81.9 1.0 %copy.16 = f32[512,512]{1,0:T(8,128)} copy(f32[512,512]{1,0:T(8,128)S(1)} %get-tuple-element.54) | data formatting | bytes 2097152
  (1 shorter events, 0.0 us)
Async XLA Ops:
  0.6 80.6 %copy-start = (bf16[1536,1024]{1,0:T(8,128)(2,1)S(1)}, bf16[1536,1024]{1,0:T(8,128)(2,1)}, u32[]{:S(2)}) copy-start(bf16[1536,1024]{1,0:T(8,128)(2,1)} %x_hbm.1) | copy-start | bytes 9437188
  0.6 80.6 %copy-start.3 = (s32[256,16]{0,1:T(8,128)S(1)}, s32[256,16]{0,1:T(8,128)}, u32[]{:S(2)}) copy-start(s32[256,16]{0,1:T(8,128)} %param.11) | copy-start | bytes 49156
  0.7 80.6 %copy-start.2 = (s32[2048,8]{0,1:T(8,128)S(1)}, s32[2048,8]{0,1:T(8,128)}, u32[]{:S(2)}) copy-start(s32[2048,8]{0,1:T(8,128)} %param.10) | copy-start | bytes 196612
  0.7 80.6 %copy-start.1 = (bf16[512,512]{1,0:T(8,128)(2,1)S(1)}, bf16[512,512]{1,0:T(8,128)(2,1)}, u32[]{:S(2)}) copy-start(bf16[512,512]{1,0:T(8,128)(2,1)} %param.9) | copy-start | bytes 1572868
  0.7 80.6 %copy-start.4 = (f32[1536]{0:T(1024)S(1)}, f32[1536]{0:T(1024)}, u32[]{:S(2)}) copy-start(f32[1536]{0:T(1024)} %param.8) | copy-start | bytes 18436

commit v4 on v3

--- a/solution.py
+++ b/solution.py
@@ -16,7 +16,10 @@
 WIDTH = KNZ * BS
 COLS = ACT * BS
 CHUNK = 256
+NBLK = 2048
 HALO = 1
+CAP = 7
+AHEAD = 4
 MESH = pl.DeviceIdType.MESH
 F32 = jnp.float32
 BF16 = jnp.bfloat16
@@ -307,12 +310,35 @@
     return 1 - lax.rem(i, 2), dz
 
 
+def fill_slot(slots, slot, source, pick, masks):
+    low, high = masks
+    for q in range(CAP // 2):
+        slots[slot, q * BS : (q + 1) * BS] = two_blocks(source, *pick(2 * q), *pick(2 * q + 1), masks)
+    row, block = pick(CAP - 1)
+    a = source[block & 1, row, block >> 1]
+    b = source[1 - (block & 1), row, block >> 1]
+    half = BS // 2
+    slots[slot, CAP // 2 * BS :] = a[:half] * low[:half] + b[half:] * high[half:]
+
+
+def open_slot(target, slots, slot):
+    for q in range(CAP // 2):
+        keep_both(target, slot, q, slots[slot, q * BS : (q + 1) * BS])
+    part = slots[slot, CAP // 2 * BS :]
+    swapped = swap_halves(part.astype(F32)).astype(BF16)
+    half = BS // 2
+    target[0, slot, CAP // 2, :half] = part
+    target[0, slot, CAP // 2, half:] = swapped
+    target[1, slot, CAP // 2, :half] = swapped
+    target[1, slot, CAP // 2, half:] = part
+
+
 def packed_kernel(
-    act, pat, weights, x_hbm, d_hbm,
+    act, pat_hbm, weights, x_hbm, d_hbm,
     dens_out, ham_out, flag_out,
     xv, xt, own, halo_d, ext2, send_d, recv_d, rows2, dfull, svec, hrows, send_h,
     recv_h, hvar, expanded, halo_out, halo_in, row_flags, region_flags,
-    halo_src, row_map, back_map, tab_row, tab_src, tab_pos,
+    pat, halo_src, row_map, back_map, tab_row, tab_src, tab_pos,
     tab_j, tab_rank, tab_local, tab_q, tab_start, tab_owner, tab_dpos, tab_h, tab_turn, tab_place, tab_order,
     local_sems, halo_send, halo_recv, a2a_send, a2a_recv, flag_send, flag_recv,
 ):
@@ -332,7 +358,9 @@
 
     x_copy = pltpu.make_async_copy(x_hbm, xv, local_sems.at[0])
     d_copy = pltpu.make_async_copy(d_hbm, own, local_sems.at[1])
+    pat_copy = pltpu.make_async_copy(pat_hbm, pat, local_sems.at[2])
     d_copy.start()
+    pat_copy.start()
     x_copy.start()
 
     barrier = pltpu.get_barrier_semaphore()
@@ -415,7 +443,7 @@
             blocks[0] = jnp.where(mine & (count == 0), ids[e], blocks[0])
             blocks[1] = jnp.where(mine & (count == 1), ids[e], blocks[1])
             count = count + mine.astype(jnp.int32)
-        packed = [jnp.int32(0)] * KNZ
+        packed = [jnp.int32(0)] * CAP
         running = jnp.int32(0)
         for c in range(2):
             group = jnp.minimum(((blocks[c] >> 7) - g + 1) & 15, 2)
@@ -427,22 +455,22 @@
                 for e in range(1, ACT):
                     gap = jnp.minimum(gap, column ^ ids[e])
                 match = (gap == 0) & valid
-                for p in range(m + 1 if c == 0 else KNZ):
+                for p in range(min(m + 1, CAP) if c == 0 else CAP):
                     packed[p] = jnp.where(match & (running == p), c * KNZ + m, packed[p])
-                tab_pos[b * 16 + c * KNZ + m] = jnp.where(match, jnp.minimum(running, KNZ - 1), KNZ)
+                tab_pos[b * 16 + c * KNZ + m] = jnp.where(match, jnp.minimum(running, CAP - 1), KNZ)
                 running = running + match.astype(jnp.int32)
-        for p in range(KNZ):
+        for p in range(CAP):
             tab_src[b * KNZ + p] = packed[p]
         tab_row[2 * ROWS + b] = count
 
     masks = half_masks()
 
     def pack_rows(b, target):
-        for q in range(KNZ // 2):
-            a = tab_src[b * KNZ + 2 * q]
-            c = tab_src[b * KNZ + 2 * q + 1]
-            target[b if target is send_d else me, q] = two_blocks(
-                ext2, tab_row[2 * b + (a >> 3)], a & 7, tab_row[2 * b + (c >> 3)], c & 7, masks)
+        def pick(p):
+            code = tab_src[b * KNZ + p]
+            return tab_row[2 * b + (code >> 3)], code & 7
+
+        fill_slot(target, b, ext2, pick, masks)
 
     def first_copy(i):
         p = peer(i)
@@ -450,7 +478,9 @@
             send_d.at[p], recv_d.at[me], a2a_send.at[i], a2a_recv.at[i],
             device_id=(g, p), device_id_type=MESH)
 
-    batch_table(peer(0))
+    pat_copy.wait()
+    for i in range(AHEAD):
+        batch_table(peer(i))
     to_right.wait_recv()
     to_left.wait_recv()
     for side in range(2):
@@ -461,11 +491,15 @@
     def send_first(i, carry):
         pack_rows(peer(i), send_d)
         first_copy(i).start()
-        following = peer(i + 1)
-        batch_table(following)
-        return carry
-
-    lax.fori_loop(0, ROWS - 1, send_first, 0)
+        return carry
+
+    def send_and_prepare(i, carry):
+        send_first(i, carry)
+        batch_table(peer(i + AHEAD))
+        return carry
+
+    lax.fori_loop(0, ROWS - AHEAD, send_and_prepare, 0)
+    lax.fori_loop(ROWS - AHEAD, ROWS - 1, send_first, 0)
     pack_rows(me, recv_d)
 
     def match_row(k, carry):
@@ -497,11 +531,11 @@
         tab_start[k] = start
         for j in range(ACT):
             local = tab_local[k * ACT + j]
-            tab_dpos[k * ACT + j] = jnp.where(local < KNZ, jnp.minimum(start + local, KNZ - 1), KNZ)
+            tab_dpos[k * ACT + j] = jnp.where(local < KNZ, jnp.minimum(start + local, CAP - 1), KNZ)
         return jnp.maximum(most, start + tab_q[k])
 
     most = lax.fori_loop(0, ACT, start_row, jnp.int32(0))
-    overflow = jnp.maximum(overflow, (most > KNZ).astype(jnp.int32))
+    overflow = jnp.maximum(overflow, (most > CAP).astype(jnp.int32))
 
     row_flags[me] = jnp.full((8, 128), overflow, jnp.int32)
 
@@ -565,16 +599,16 @@
             entries[0] = jnp.where(mine & (count == 0), k, entries[0])
             entries[1] = jnp.where(mine & (count == 1), k, entries[1])
             count = count + mine.astype(jnp.int32)
-        packed = [jnp.int32(0)] * KNZ
+        packed = [jnp.int32(0)] * CAP
         for c in range(2):
             k = entries[c]
             start = jnp.where(count > c, tab_start[k], 64)
             for m in range(KNZ):
                 place = start + tab_rank[k * KNZ + m]
                 code = tab_place[k] * ACT + jnp.minimum(tab_j[k * KNZ + m], ACT - 1)
-                for p in range(m + 1 if c == 0 else KNZ):
+                for p in range(min(m + 1, CAP) if c == 0 else CAP):
                     packed[p] = jnp.where(place == p, code, packed[p])
-        for p in range(KNZ):
+        for p in range(CAP):
             tab_h[r * KNZ + p] = packed[p]
         return carry
 
@@ -596,8 +630,7 @@
     lax.fori_loop(0, PTS // 128, transpose_chunk, 0)
 
     def spread_slot(r):
-        for q in range(KNZ // 2):
-            keep_both(rows2, r, q, recv_d[r, q])
+        open_slot(rows2, recv_d, r)
 
     spread_slot(me)
 
@@ -646,11 +679,12 @@
     region_flags[0, 0] = merged
     region_flag_copy(0).start()
 
-    def pack_slot(r, target, target_row):
-        for q in range(KNZ // 2):
-            a = tab_h[r * KNZ + 2 * q]
-            b = tab_h[r * KNZ + 2 * q + 1]
-            target[target_row, q] = two_blocks(hrows, a >> 4, a & 15, b >> 4, b & 15, masks)
+    def pack_slot(r, target):
+        def pick(p):
+            code = tab_h[r * KNZ + p]
+            return code >> 4, code & 15
+
+        fill_slot(target, r, hrows, pick, masks)
 
     def second_copy(i):
         p = peer(i)
@@ -660,7 +694,7 @@
 
     def send_second(i, carry):
         p = peer(i)
-        pack_slot(p, send_h, p)
+        pack_slot(p, send_h)
         second_copy(i).start()
         return carry
 
@@ -683,15 +717,14 @@
 
     lax.fori_loop(0, COLS // CHUNK, ham_chunk, 0)
     lax.fori_loop(2 * (COLS // CHUNK), ROWS - 1, send_second, 0)
-    pack_slot(me, recv_h, me)
+    pack_slot(me, recv_h)
 
     merge_flags(0)
     merge_flags(1)
     merge_flags(2)
 
     def expand_slot(b):
-        for q in range(KNZ // 2):
-            keep_both(hvar, b, q, recv_h[b, q])
+        open_slot(hvar, recv_h, b)
         for c in range(2):
             for q in range(KNZ // 2):
                 expanded[2 * b + c, q] = pair_of_blocks(
@@ -824,6 +857,7 @@
 def packed_capacity(act, pat, weights, x, d):
     in_specs, vmem = specs()
     half = KNZ // 2
+    in_specs[1] = in_specs[3]
     return pl.pallas_call(
         packed_kernel,
         out_shape=(
@@ -839,20 +873,21 @@
             pltpu.VMEM((BLK_DEV, BS, WIDTH), BF16),
             pltpu.VMEM((2, HALO, BS, WIDTH), BF16),
             pltpu.VMEM((2, BLK_DEV + 2 * HALO, half, BS, 128), BF16),
-            pltpu.VMEM((ROWS, half, BS, 128), BF16),
-            pltpu.VMEM((ROWS, half, BS, 128), BF16),
+            pltpu.VMEM((ROWS, CAP * BS // 2, 128), BF16),
+            pltpu.VMEM((ROWS, CAP * BS // 2, 128), BF16),
             pltpu.VMEM((2, ROWS, half + 1, BS, 128), BF16),
             pltpu.VMEM((COLS, COLS), BF16),
             pltpu.VMEM((1, PTS), F32),
             pltpu.VMEM((2, ACT, ACT // 2, BS, 128), BF16),
-            pltpu.VMEM((ROWS, half, BS, 128), BF16),
-            pltpu.VMEM((ROWS, half, BS, 128), BF16),
+            pltpu.VMEM((ROWS, CAP * BS // 2, 128), BF16),
+            pltpu.VMEM((ROWS, CAP * BS // 2, 128), BF16),
             pltpu.VMEM((2, ROWS, half + 1, BS, 128), BF16),
             pltpu.VMEM((2 * ROWS + 1, half, BS, 128), BF16),
             pltpu.VMEM((2, HALO, BS, WIDTH), BF16),
             pltpu.VMEM((2, HALO + 1, BS, WIDTH), BF16),
             pltpu.VMEM((ROWS, 8, 128), jnp.int32),
             pltpu.VMEM((2, 4, 8, 128), jnp.int32),
+            pltpu.SMEM((KNZ, NBLK), jnp.int32),
             pltpu.SMEM((2 * HALO,), jnp.int32),
             pltpu.SMEM((3 * BLK_DEV,), jnp.int32),
             pltpu.SMEM((2 * BLK_DEV,), jnp.int32),
@@ -870,7 +905,7 @@
             pltpu.SMEM((ROWS,), jnp.int32),
             pltpu.SMEM((ACT,), jnp.int32),
             pltpu.SMEM((ACT,), jnp.int32),
-            pltpu.SemaphoreType.DMA((2,)),
+            pltpu.SemaphoreType.DMA((3,)),
             pltpu.SemaphoreType.DMA((4,)),
             pltpu.SemaphoreType.DMA((4,)),
             pltpu.SemaphoreType.DMA((30,)),

time: 83.3 us -> 77 us (0.924)
  Pallas kernels: 79.9 us -> 73.8 us
    pallas_call x1, Pallas kernels: 79.9 us -> 73.8 us  [packed_capacity(): pl.pallas_call(packed_kernel, out_shape=(jax.ShapeDtypeStruct((PTS // 128...]
where the time goes in v4:
time: 77 us; the launch traced here: 76.9 us
  Pallas kernels  73.8 us (96%)
  local copies, waits for them, and re-layouts  1.59 us (2%)
  between operations  1.35 us (2%)
    pallas_call x1, Pallas kernels, packed_capacity(): pl.pallas_call(packed_kernel, out_shape=(jax.ShapeDtypeStruct((PTS // 128...  73.8 us
    unnamed x12, local copies, waits for them, and re-layouts  1.59 us

profile of v4, /device:TPU:1, one launch (start us, length us, event | category | flops | bytes accessed | tf_op | source)
XLA Modules:
  0.0 76.9 jit_solution(2970052326905940691)
XLA Ops:
  0.6 0.0 copy-start
  0.6 0.0 copy-start.3
  0.7 0.0 copy-start.2
  0.7 0.0 copy-start.1
  0.7 0.0 copy-start.4
  0.7 73.8 %shard_map.68 = (f32[12,128]{1,0:T(8,128)S(1)}, f32[8,64,512]{2,1,0:T(8,128)S(1)}, s32[1,1]{1,0:T(1,128)}) custom-call(s32[16,256]{1,0:T(8,128)} %bitcast.15, s32[8,2048]{1,0:T(8,128)} %bitcast.13, f32[12,128]{1,0:T(8,128)} %bitcast.17, bf16[1536,1024]{1,0:T(8,128)(2,1)} %x_hbm.1, bf16[8,64,512]{2,1,0:T(8,128)(2,1)} %bitcast.9), custom_call_target="tpu_custom_call" | custom-call | tf_op jit(solution)/shard_map/pallas_call | solution.py:861
  75.1 0.0 copy-done
  75.1 0.0 copy-done.3
  75.1 0.0 copy-done.2
  75.2 0.0 copy-done.1
  75.2 0.0 copy-done.4
  75.2 0.2 conditional.1
  75.4 0.6 copy.15
  76.0 1.0 %copy.16 = f32[512,512]{1,0:T(8,128)} copy(f32[512,512]{1,0:T(8,128)S(1)} %get-tuple-element.54) | data formatting | bytes 2097152
Async XLA Ops:
  0.6 74.5 %copy-start = (bf16[1536,1024]{1,0:T(8,128)(2,1)S(1)}, bf16[1536,1024]{1,0:T(8,128)(2,1)}, u32[]{:S(2)}) copy-start(bf16[1536,1024]{1,0:T(8,128)(2,1)} %x_hbm.1) | copy-start | bytes 9437188
  0.6 74.5 %copy-start.3 = (s32[256,16]{0,1:T(8,128)S(1)}, s32[256,16]{0,1:T(8,128)}, u32[]{:S(2)}) copy-start(s32[256,16]{0,1:T(8,128)} %param.11) | copy-start | bytes 49156
  0.7 74.5 %copy-start.2 = (s32[2048,8]{0,1:T(8,128)S(1)}, s32[2048,8]{0,1:T(8,128)}, u32[]{:S(2)}) copy-start(s32[2048,8]{0,1:T(8,128)} %param.10) | copy-start | bytes 196612
  0.7 74.5 %copy-start.1 = (bf16[512,512]{1,0:T(8,128)(2,1)S(1)}, bf16[512,512]{1,0:T(8,128)(2,1)}, u32[]{:S(2)}) copy-start(bf16[512,512]{1,0:T(8,128)(2,1)} %param.9) | copy-start | bytes 1572868
  0.7 74.5 %copy-start.4 = (f32[1536]{0:T(1024)S(1)}, f32[1536]{0:T(1024)}, u32[]{:S(2)}) copy-start(f32[1536]{0:T(1024)} %param.8) | copy-start | bytes 18436

commit v5 on v4

--- a/solution.py
+++ b/solution.py
@@ -20,6 +20,7 @@
 HALO = 1
 CAP = 7
 AHEAD = 4
+POINTS = 512
 MESH = pl.DeviceIdType.MESH
 F32 = jnp.float32
 BF16 = jnp.bfloat16
@@ -305,6 +306,7 @@
 
 
 def offset_of(i):
+    i = lax.rem(i, 8) * 2 + lax.div(i, 8)
     j = lax.div(i, 2)
     dz = 4 + lax.div(j + 1, 2) * (1 - 2 * lax.rem(j, 2))
     return 1 - lax.rem(i, 2), dz
@@ -651,22 +653,22 @@
     lax.fori_loop(0, ACT, assemble_row, 0)
 
     def density_chunk(i, carry):
-        points = pl.ds(pl.multiple_of(i * CHUNK, CHUNK), CHUNK)
+        points = pl.ds(pl.multiple_of(i * POINTS, POINTS), POINTS)
         x = xv[points, :]
-        part = jnp.zeros((CHUNK, 128), F32)
+        part = jnp.zeros((POINTS, 128), F32)
         for n in range(COLS // CHUNK):
             product = jnp.dot(x, dfull[:, n * CHUNK : (n + 1) * CHUNK], preferred_element_type=F32)
             product = product * x[:, n * CHUNK : (n + 1) * CHUNK].astype(F32)
             part = part + (product[:, :128] + product[:, 128:])
         dens = jnp.sum(jnp.transpose(part), axis=0, keepdims=True)
-        for half in range(CHUNK // 128):
-            row = pl.ds(i * (CHUNK // 128) + half, 1)
+        for half in range(POINTS // 128):
+            row = pl.ds(i * (POINTS // 128) + half, 1)
             dens_half = dens[:, half * 128 : (half + 1) * 128]
             dens_out[row, :] = dens_half
-            svec[:, pl.ds(pl.multiple_of(i * CHUNK + half * 128, 128), 128)] = weights[row, :] * jnp.tanh(dens_half)
-        return carry
-
-    lax.fori_loop(0, PTS // CHUNK, density_chunk, 0)
+            svec[:, pl.ds(pl.multiple_of(i * POINTS + half * 128, 128), 128)] = weights[row, :] * jnp.tanh(dens_half)
+        return carry
+
+    lax.fori_loop(0, PTS // POINTS, density_chunk, 0)
 
     def take_flag(i, carry):
         row_flag_copy(i).wait_recv()

time: 77 us -> 75.3 us (0.978)
  Pallas kernels: 73.8 us -> 72.1 us
    pallas_call x1, Pallas kernels: 73.8 us -> 72.1 us  [packed_capacity(): pl.pallas_call(packed_kernel, out_shape=(jax.ShapeDtypeStruct((PTS // 128...]
where the time goes in v5:
time: 75.3 us; the launch traced here: 75.2 us
  Pallas kernels  72.1 us (96%)
  local copies, waits for them, and re-layouts  1.59 us (2%)
  between operations  1.35 us (2%)
    pallas_call x1, Pallas kernels, packed_capacity(): pl.pallas_call(packed_kernel, out_shape=(jax.ShapeDtypeStruct((PTS // 128...  72.1 us
    unnamed x12, local copies, waits for them, and re-layouts  1.59 us

profile of v5, /device:TPU:1, one launch (start us, length us, event | category | flops | bytes accessed | tf_op | source)
XLA Modules:
  0.0 75.2 jit_solution(13271374325039492147)
XLA Ops:
  0.6 0.0 copy-start
  0.6 0.0 copy-start.3
  0.7 0.0 copy-start.2
  0.7 0.0 copy-start.1
  0.7 0.0 copy-start.4
  0.7 72.1 %shard_map.68 = (f32[12,128]{1,0:T(8,128)S(1)}, f32[8,64,512]{2,1,0:T(8,128)S(1)}, s32[1,1]{1,0:T(1,128)}) custom-call(s32[16,256]{1,0:T(8,128)} %bitcast.15, s32[8,2048]{1,0:T(8,128)} %bitcast.13, f32[12,128]{1,0:T(8,128)} %bitcast.17, bf16[1536,1024]{1,0:T(8,128)(2,1)} %x_hbm.1, bf16[8,64,512]{2,1,0:T(8,128)(2,1)} %bitcast.9), custom_call_target="tpu_custom_call" | custom-call | tf_op jit(solution)/shard_map/pallas_call | solution.py:863
  73.4 0.0 copy-done
  73.4 0.0 copy-done.3
  73.4 0.0 copy-done.2
  73.4 0.0 copy-done.1
  73.4 0.0 copy-done.4
  73.4 0.2 conditional.1
  73.6 0.6 copy.15
  74.2 1.0 %copy.16 = f32[512,512]{1,0:T(8,128)} copy(f32[512,512]{1,0:T(8,128)S(1)} %get-tuple-element.54) | data formatting | bytes 2097152
Async XLA Ops:
  0.6 72.8 %copy-start = (bf16[1536,1024]{1,0:T(8,128)(2,1)S(1)}, bf16[1536,1024]{1,0:T(8,128)(2,1)}, u32[]{:S(2)}) copy-start(bf16[1536,1024]{1,0:T(8,128)(2,1)} %x_hbm.1) | copy-start | bytes 9437188
  0.6 72.8 %copy-start.3 = (s32[256,16]{0,1:T(8,128)S(1)}, s32[256,16]{0,1:T(8,128)}, u32[]{:S(2)}) copy-start(s32[256,16]{0,1:T(8,128)} %param.11) | copy-start | bytes 49156
  0.7 72.8 %copy-start.2 = (s32[2048,8]{0,1:T(8,128)S(1)}, s32[2048,8]{0,1:T(8,128)}, u32[]{:S(2)}) copy-start(s32[2048,8]{0,1:T(8,128)} %param.10) | copy-start | bytes 196612
  0.7 72.8 %copy-start.1 = (bf16[512,512]{1,0:T(8,128)(2,1)S(1)}, bf16[512,512]{1,0:T(8,128)(2,1)}, u32[]{:S(2)}) copy-start(bf16[512,512]{1,0:T(8,128)(2,1)} %param.9) | copy-start | bytes 1572868
  0.7 72.8 %copy-start.4 = (f32[1536]{0:T(1024)S(1)}, f32[1536]{0:T(1024)}, u32[]{:S(2)}) copy-start(f32[1536]{0:T(1024)} %param.8) | copy-start | bytes 18436
